TPU v7x, 512 devices: a whole 4x4x16 slice. The times are simulated.
512 devices in a mesh: xt: 32 (over z_lo, x, core), yt: 16 (over z_hi, y).
Axes of the slice: x: 4, y: 4, z: 16 (z_hi: 4, z_lo: 4; z = z_hi * 4 + z_lo), core: 2. Of those that a mesh axis runs over, the one named last changes fastest.
Arguments:
- cotangent: bfloat16 [512, 512, 1024], P('xt', 'yt'), may hold values from -6 to 6
- preact: bfloat16 [512, 512, 1024], P('xt', 'yt'), may hold values from -8 to 8
- spectra: float32 [32, 32, 512], P('xt', 'yt'), may hold values from -6 to 6
- spectral_weight: float32 [32, 32, 8192], P('xt', 'yt'), may hold values from -12 to 12
- local_weight: bfloat16 [16, 16], replicated, may hold values from -1.5 to 1.5
Outputs:
- grad_input: float32 [512, 512, 1024], P('xt', 'yt')
- grad_weight: float32 [32, 32, 8192], P('xt', 'yt')
All inputs are finite; a program needn't handle non-finite values.
Results may differ from a plain program's by a relative error of at most 0.0034.
Values may be sent and summed in bfloat16 or wider, within the bound.
No kernel may reach another device: no remote copies, remote signals or barrier semaphores. Data moves between devices by JAX's collectives and lax.ppermute only.
A program may use at most 64 MiB of HBM per device.

v0:
```python
import math

import jax
import jax.numpy as jnp
from jax import lax
from jax.sharding import PartitionSpec as P

PRECISE = lax.Precision.HIGHEST


def mode_ids(mode_count, length):
    ordinal = jnp.arange(mode_count, dtype=jnp.int32)
    return jnp.where(ordinal < mode_count // 2, ordinal, ordinal + (length - mode_count))


def phase_pair(positions, mode_list, length):
    product = positions[:, None] * mode_list[None, :] % length
    phase_angle = product.astype(jnp.float32) * (2.0 * math.pi / length)
    return (jnp.cos(phase_angle), jnp.sin(phase_angle))


def gelu_slope(pre_value):
    normal_cdf = 0.5 * (1.0 + jax.scipy.special.erf(pre_value * (1.0 / math.sqrt(2.0))))
    return normal_cdf + pre_value * jnp.exp(-0.5 * pre_value * pre_value) * (
        1.0 / math.sqrt(2.0 * math.pi)
    )


def slope_grad(cotangent, preact):
    pre_value = preact.astype(jnp.float32)
    return (cotangent.astype(jnp.float32) * gelu_slope(pre_value)).astype(jnp.bfloat16)


def rotate_sum(data, cosine_table, sine_table, form, direction):
    half_width = data.shape[-1] // 2
    real_part = data[..., :half_width]
    imaginary = data[..., half_width:]

    def contract(operand, factor):
        return jnp.einsum(form, operand, factor, precision=PRECISE)

    new_real = contract(real_part, cosine_table) - direction * contract(imaginary, sine_table)
    new_imaginary = contract(imaginary, cosine_table) + direction * contract(real_part, sine_table)
    return jnp.concatenate([new_real, new_imaginary], axis=-1)


def forward_depth(grid_depth, mode_count):
    cosine_table, sine_table = phase_pair(
        jnp.arange(grid_depth, dtype=jnp.int32), jnp.arange(mode_count, dtype=jnp.int32), grid_depth
    )
    weighting = jnp.where(jnp.arange(mode_count) == 0, 1.0, 2.0).astype(jnp.float32)
    return jnp.stack([cosine_table * weighting, -sine_table * weighting], axis=1).astype(
        jnp.bfloat16
    )


def inverse_depth(grid_depth, mode_count):
    cosine_table, sine_table = phase_pair(
        jnp.arange(grid_depth, dtype=jnp.int32), jnp.arange(mode_count, dtype=jnp.int32), grid_depth
    )
    return jnp.stack([cosine_table.T, -sine_table.T], axis=0)


def depth_project(grad_pre, factor_table, channels):
    tile_rows, tile_columns, row_width = grad_pre.shape
    grid_depth = row_width // channels
    grid_cells = grad_pre.reshape(tile_rows, tile_columns, grid_depth, channels)
    result = jnp.einsum(
        "xyzc,zrk->xyrkc", grid_cells, factor_table, preferred_element_type=jnp.float32
    )
    return result.reshape(tile_rows, tile_columns, -1)


def depth_expand(data, factor_table, channels):
    tile_rows, tile_columns, row_width = data.shape
    mode_count = factor_table.shape[1]
    mode_cells = data.reshape(tile_rows, tile_columns, 2, mode_count, channels)
    result = jnp.einsum("xyrkc,rkz->xyzc", mode_cells, factor_table, precision=PRECISE)
    return result.reshape(tile_rows, tile_columns, -1)


def mode_update(mode_grad, spectra, spectral_weight, mode_count, channels):
    lead_first, lead_second = (mode_grad.shape[0], mode_grad.shape[1])
    gradient = mode_grad.reshape(lead_first, lead_second, 2, mode_count, channels)
    saved = spectra.reshape(lead_first, lead_second, 2, mode_count, channels)
    weights = spectral_weight.reshape(lead_first, lead_second, 2, mode_count, channels, channels)
    grad_real, grad_imaginary = (gradient[:, :, 0], gradient[:, :, 1])
    saved_real, saved_imaginary = (saved[:, :, 0], saved[:, :, 1])
    weight_real, weight_imaginary = (weights[:, :, 0], weights[:, :, 1])
    outer_real = (
        saved_real[..., :, None] * grad_real[..., None, :]
        + saved_imaginary[..., :, None] * grad_imaginary[..., None, :]
    )
    outer_imaginary = (
        saved_real[..., :, None] * grad_imaginary[..., None, :]
        - saved_imaginary[..., :, None] * grad_real[..., None, :]
    )
    grad_weight = jnp.stack([outer_real, outer_imaginary], axis=2).reshape(
        lead_first, lead_second, -1
    )

    def contract(matrix, vector):
        return jnp.einsum("abkco,abko->abkc", matrix, vector, precision=PRECISE)

    back_real = contract(weight_real, grad_real) + contract(weight_imaginary, grad_imaginary)
    back_imaginary = contract(weight_real, grad_imaginary) - contract(weight_imaginary, grad_real)
    spectra_grad = (
        jnp.stack([back_real, back_imaginary], axis=2)
        .reshape(lead_first, lead_second, -1)
        .astype(jnp.bfloat16)
    )
    return (grad_weight, spectra_grad)


def on_device(cotangent, preact, spectra, spectral_weight, local_weight):
    tile_rows, tile_columns, row_width = cotangent.shape
    channels = local_weight.shape[0]
    grid_depth = row_width // channels
    devices_first = lax.axis_size("xt")
    devices_second = lax.axis_size("yt")
    block_first, block_second = (spectra.shape[0], spectra.shape[1])
    modes_first = block_first * devices_first
    modes_second = block_second * devices_second
    mode_count = spectra.shape[2] // (2 * channels)
    cells_first = tile_rows * devices_first
    cells_second = tile_columns * devices_second
    norm_factor = 1.0 / math.sqrt(cells_first * cells_second * grid_depth)
    place_first = lax.axis_index("xt") * tile_rows + jnp.arange(tile_rows, dtype=jnp.int32)
    place_second = lax.axis_index("yt") * tile_columns + jnp.arange(tile_columns, dtype=jnp.int32)
    cosine_first, sine_first = phase_pair(
        place_first, mode_ids(modes_first, cells_first), cells_first
    )
    cosine_second, sine_second = phase_pair(
        place_second, mode_ids(modes_second, cells_second), cells_second
    )
    grad_pre = slope_grad(cotangent, preact)
    depth_data = depth_project(grad_pre, forward_depth(grid_depth, mode_count), channels)
    after_second = rotate_sum(depth_data, cosine_second, sine_second, "xyf,yj->xjf", -1.0)
    after_first = rotate_sum(after_second, cosine_first, sine_first, "xjf,xi->ijf", -1.0)
    features = after_first.shape[-1]
    ordered = after_first.reshape(
        devices_first, block_first, devices_second, block_second, features
    )
    ordered = ordered.transpose(0, 2, 1, 3, 4).reshape(-1, features)
    summed = lax.psum_scatter(ordered, ("xt", "yt"), scatter_dimension=0, tiled=True)
    mode_grad = summed.reshape(block_first, block_second, features) * norm_factor
    grad_weight, spectra_grad = mode_update(
        mode_grad, spectra, spectral_weight, mode_count, channels
    )
    cells_view = grad_pre.reshape(tile_rows, tile_columns, grid_depth, channels)
    local_part = jnp.einsum(
        "xyzo,co->xyzc", cells_view, local_weight, preferred_element_type=jnp.float32
    )
    local_part = local_part.reshape(tile_rows, tile_columns, -1)
    features = spectra_grad.shape[-1]
    pieces = lax.all_gather(
        spectra_grad.reshape(block_first * block_second, features), ("xt", "yt"), axis=0, tiled=True
    )
    all_modes = pieces.reshape(devices_first, devices_second, block_first, block_second, features)
    all_modes = all_modes.transpose(0, 2, 1, 3, 4).reshape(modes_first, modes_second, features)
    expanded_first = rotate_sum(
        all_modes.astype(jnp.float32), cosine_first, sine_first, "ijf,xi->xjf", 1.0
    )
    expanded_second = rotate_sum(expanded_first, cosine_second, sine_second, "xjf,yj->xyf", 1.0)
    spectral_part = (
        depth_expand(expanded_second, inverse_depth(grid_depth, mode_count), channels) * norm_factor
    )
    return (spectral_part + local_part, grad_weight)


def solution(mesh):
    in_specs = (
        P("xt", "yt", None),
        P("xt", "yt", None),
        P("xt", "yt", None),
        P("xt", "yt", None),
        P(),
    )
    out_specs = (P("xt", "yt", None), P("xt", "yt", None))
    return jax.shard_map(
        on_device, mesh=mesh, in_specs=in_specs, out_specs=out_specs, check_vma=False
    )
```

profile of v0, /device:TPU:1, one launch (start us, length us, event | category | flops | bytes accessed | tf_op | source)
XLA Modules:
  0.0 1610.2 jit_solution(7834469626701894593)
XLA Ops:
  7.2 0.0 copy-start
  7.2 0.0 all-reduce.3.cloned.1.call-start
  7.2 2.2 fusion.12
  9.5 3.2 copy.49
  12.7 4.9 copy.50
  17.6 0.1 multiply_convert_fusion.1
  17.7 3.2 convolution_bitcast_fusion
  20.9 3.7 copy.51
  24.6 0.0 copy-start.2
  24.6 4.1 fusion.23
  28.7 4.0 fusion.38
  32.7 0.0 copy-done.2
  32.7 2.4 fusion.35
  35.1 4.0 fusion.29
  39.1 1.3 fusion.49
  40.4 1.5 fusion.53
  41.9 1.3 fusion.21
  43.2 1.3 fusion.22
  44.6 0.3 pad_maximum_fusion
  44.8 2.5 copy.62
  47.4 0.0 copy-start.3
  47.4 0.0 all-reduce.3.cloned.1.call-update
  47.4 0.0 all-gather.3.cloned.1.call-start
  47.5 0.8 copy-done.3
  48.2 0.2 reshape.318
  48.5 480.6 %all-reduce.3.cloned.1.call-done = f32[1024,512]{1,0:T(8,128)} async-done(((f32[1024,512]{1,0:T(8,128)}), f32[1024,512]{1,0:T(8,128)}) %all-reduce.3.cloned.1.call-update) | async-done | bytes 2097168
  529.1 0.7 dynamic-slice_multiply_fusion
  529.8 0.1 reshape.316
  529.9 0.5 fusion.63
  530.4 0.5 fusion.62
  530.9 0.5 fusion.61
  531.5 0.5 fusion.64
  532.0 0.7 reshape.325
  532.7 0.0 all-gather.3.cloned.1.call-update
  532.7 0.0 copy-done
  532.7 6.6 fusion.115
  539.4 0.0 copy-start.4
  539.4 7.2 copy.72
  546.5 0.0 copy-done.4
  546.5 0.1 reshape.323
  546.6 0.1 sine_negate_fusion
  546.7 0.2 multiply_add_fusion
  546.9 0.9 reshape.324
  547.9 1019.3 %all-gather.3.cloned.1.call-done = bf16[512,2,512]{2,1,0:T(2,128)(2,1)} async-done(((bf16[1,2,512]{2,1,0:T(2,128)(2,1)}), bf16[512,2,512]{2,1,0:T(2,128)(2,1)}) %all-gather.3.cloned.1.call-update) | async-done | bytes 1048592 | tf_op jit(solution)/shard_map/all_gather | solution.py:156
  1567.2 1.5 reshape_transpose_reshape.7
  1568.7 0.1 fusion.194
  1568.8 0.7 fusion.55
  1569.5 0.7 fusion.59
  1570.2 0.7 convolution_add_fusion.1
  1570.8 1.0 fusion.43
  1571.8 0.7 convolution_subtract_fusion.1
  1572.5 1.0 fusion.47
  1573.5 1.0 fusion.41
  1574.5 1.0 fusion.42
  1575.5 0.1 pad_maximum_fusion.1
  1575.6 2.7 copy.69
  1578.3 11.6 bitcast_add_fusion
  1589.9 7.2 copy.73
  1597.1 0.0 copy-start.1
  1597.1 6.3 copy.74
  1603.3 0.0 copy-done.1
  (9 shorter events, 0.1 us)
Async XLA Ops:
  7.2 525.6 %copy-start = (bf16[16,16]{1,0:T(8,128)(2,1)S(1)}, bf16[16,16]{1,0:T(8,128)(2,1)}, u32[]{:S(2)}) copy-start(bf16[16,16]{1,0:T(8,128)(2,1)} %param.9) | copy-start | bytes 1540
  7.2 521.9 %all-reduce.3.cloned.1.call-start = ((), (), s32[]{:S(2)}) async-start(), calls=%async_computation.1 | async-start | bytes 4194304
  24.6 8.1 copy-start.2
  47.4 0.8 copy-start.3
  47.4 1519.8 %all-gather.3.cloned.1.call-start = ((), (), s32[]{:S(2)}) async-start(), calls=%async_computation | async-start | bytes 1050624 | tf_op jit(solution)/shard_map/all_gather | solution.py:156
  539.4 7.2 copy-start.4
  1597.1 6.3 copy-start.1
Sparse Core Ops, SparseCore 0:
  47.5 481.4 all-reduce.2
  532.9 1034.3 all-gather.2
where the time goes:
time: 1610 us
  waiting for transfers between devices  1500 us (93%)
  matrix products  50 us (3%)
  local copies, waits for them, and re-layouts  42 us (3%)
    all_gather x1, waiting for transfers between devices, on_device(): lax.all_gather(spectra_grad.reshape(block_first * block_second, features)...  1020 us
    unnamed x3, waiting for transfers between devices  481 us
  transfers between devices with their start and end apart: 2, of which 2 were waited for; matrix products, arithmetic and copies ran while one was open for 1% of the time, Pallas kernels for 0%

commit v1 on v0

v1 whole, which is shorter than its diff:
```python
import functools
import math

import jax
import jax.numpy as jnp
import ml_dtypes
import numpy as np
from jax import lax
from jax.experimental import pallas as pl
from jax.experimental.pallas import tpu as pltpu
from jax.sharding import Mesh
from jax.sharding import PartitionSpec as P

TILE_X, TILE_Y, DEPTH, CH = 16, 32, 64, 16
KX, KY, KZ = 32, 32, 16
NX, NY = 512, 512
ZL, XS, CS, ZH, YS = 4, 4, 2, 4, 4
ROW = DEPTH * CH
HALF = KZ * CH
STEPS = 4
STEP_X = TILE_X // STEPS
STEP_ROWS = STEP_X * TILE_Y
F32, BF16 = jnp.float32, jnp.bfloat16
MIB = 1024 * 1024


def split_table(table):
    high = table.astype(ml_dtypes.bfloat16)
    low = (table - high.astype(np.float64)).astype(ml_dtypes.bfloat16)
    return high, low


def mode_ids(count, length):
    ordinal = np.arange(count)
    return np.where(ordinal < count // 2, ordinal, ordinal + length - count)


def phase(positions, modes, length):
    angle = (np.outer(modes, positions) % length) * (2.0 * np.pi / length)
    return np.cos(angle), np.sin(angle)


KX_ORDER = np.array([zl * 8 + x * 2 + c for x in range(XS) for c in range(CS) for zl in range(ZL)])


def place_of(ky):
    return ky // 8, ky % 8 // 2, ky % 2


@functools.cache
def tables():
    ky = mode_ids(KY, NY)
    kx = mode_ids(KX, NX)[KX_ORDER]
    forward_y, inverse_y, forward_x, inverse_x = [], [], [], []
    for tile in range(NY // TILE_Y):
        cosine, sine = phase(tile * TILE_Y + np.arange(TILE_Y), ky, NY)
        rows = np.stack(
            [np.concatenate([cosine, sine], 1), np.concatenate([-sine, cosine], 1)], 1
        ).reshape(2 * KY, 2 * TILE_Y)
        high, low = split_table(rows)
        forward_y.append(np.concatenate([high, high, low], 1))
        rows = np.concatenate(
            [np.concatenate([cosine.T, -sine.T], 1), np.concatenate([sine.T, cosine.T], 1)], 0
        )
        high, low = split_table(rows)
        inverse_y.append(np.concatenate([high, high, low], 1))
    for tile in range(NX // TILE_X):
        cosine, sine = phase(tile * TILE_X + np.arange(TILE_X), kx, NX)
        rows = np.concatenate(
            [np.concatenate([cosine, sine], 1), np.concatenate([-sine, cosine], 1)], 0
        )
        high, low = split_table(rows)
        forward_x.append(np.concatenate([high, high, low], 1))
        rows = np.concatenate(
            [np.concatenate([cosine.T, -sine.T], 1), np.concatenate([sine.T, cosine.T], 1)], 0
        )
        high, low = split_table(rows)
        inverse_x.append(np.concatenate([high, low], 1))
    depth_angle = (np.outer(np.arange(DEPTH), np.arange(KZ)) % DEPTH) * (2.0 * np.pi / DEPTH)
    weight = np.where(np.arange(KZ) == 0, 1.0, 2.0)
    factor = np.stack([np.cos(depth_angle) * weight, -np.sin(depth_angle) * weight], 1)
    factor = factor.astype(np.float32).astype(ml_dtypes.bfloat16).astype(np.float64)
    eye = np.eye(CH)
    project = np.kron(factor.reshape(DEPTH, 2 * KZ), eye).astype(ml_dtypes.bfloat16)
    expand = np.stack([np.cos(depth_angle).T, -np.sin(depth_angle).T], 0)
    expand = np.kron(expand.reshape(2 * KZ, DEPTH), eye) / math.sqrt(NX * NY * DEPTH)
    expand_high, expand_low = split_table(expand)
    kz8, ones = np.eye(8), np.ones((1, CH))
    spread_o = np.kron(kz8, np.kron(ones, eye)).astype(ml_dtypes.bfloat16)
    spread_c = np.kron(kz8, np.kron(eye, ones)).astype(ml_dtypes.bfloat16)
    return dict(
        forward_y=np.stack(forward_y),
        inverse_y=np.stack(inverse_y),
        forward_x=np.stack(forward_x),
        inverse_x=np.stack(inverse_x),
        project=project,
        expand_high=expand_high,
        expand_low=expand_low,
        spread_o=spread_o,
        spread_c=spread_c,
    )


def dot(left, right):
    return lax.dot_general(left, right, (((1,), (0,)), ((), ())), preferred_element_type=F32)


def split(value):
    high = value.astype(BF16)
    return high, (value - high.astype(F32)).astype(BF16)


def split_rows(value):
    high, low = split(value)
    return jnp.concatenate([high, low, high], 0)


def three_parts(value):
    high = value.astype(BF16)
    rest = value - high.astype(F32)
    middle = rest.astype(BF16)
    low = (rest - middle.astype(F32)).astype(BF16)
    return jnp.concatenate([high, middle, low], 0)


def sum_parts(value):
    rows = value.shape[0] // 3
    return value[:rows] + (value[rows : 2 * rows] + value[2 * rows :])


def gelu_slope(pre_value):
    normal_cdf = 0.5 * (1.0 + lax.erf(pre_value * (1.0 / math.sqrt(2.0))))
    return normal_cdf + pre_value * jnp.exp(-0.5 * pre_value * pre_value) * (
        1.0 / math.sqrt(2.0 * math.pi)
    )


def mode_rows(ky, quarter):
    zh, y, local = place_of(ky)
    return pl.ds(y * 1024 + zh * 8 + quarter * 2 + local, KX, stride=32)


def project_kernel(
    at_ref, cot_ref, pre_ref, project_ref, fy_ref, fx_ref, slope_ref, out_ref, t_refs, p_ref
):
    step = pl.program_id(0)
    pre_value = pre_ref[...].astype(F32)
    slope = (cot_ref[...].astype(F32) * gelu_slope(pre_value)).astype(BF16)
    slope_ref[...] = slope
    depth = dot(slope, project_ref[...])
    for local in range(STEP_X):
        block = depth[local * TILE_Y : (local + 1) * TILE_Y]
        stacked = jnp.concatenate([block[:, :HALF], block[:, HALF:]], 0)
        turned = dot(fy_ref[...], split_rows(stacked))
        for half in range(2):
            t_refs[half, pl.ds(step * STEP_X + local, 2 * KY, stride=TILE_X), :] = turned[
                :, half * 128 : (half + 1) * 128
            ]

    @pl.when(step == STEPS - 1)
    def _():
        for ky in range(KY):
            rows = slice(ky * 2 * TILE_X, (ky + 1) * 2 * TILE_X)
            stacked = jnp.concatenate([t_refs[0, rows, :], t_refs[1, rows, :]], 1)
            turned = dot(fx_ref[...], split_rows(stacked))
            for part in range(2):
                for half in range(2):
                    p_ref[mode_rows(ky, part * 2 + half), :] = turned[
                        part * KX : (part + 1) * KX, half * 128 : (half + 1) * 128
                    ]
        out_ref[...] = p_ref[...].astype(BF16)


def project_call(place, cotangent, preact, table):
    def whole(shape):
        return pl.BlockSpec(shape, lambda i, at: (0, 0))

    rows = TILE_X * TILE_Y
    chunk = pl.BlockSpec((STEP_ROWS, ROW), lambda i, at: (i, 0))
    return pl.pallas_call(
        project_kernel,
        grid_spec=pltpu.PrefetchScalarGridSpec(
            num_scalar_prefetch=1,
            grid=(STEPS,),
            in_specs=[
                chunk,
                chunk,
                whole((ROW, 2 * HALF)),
                pl.BlockSpec((None, 2 * KY, 6 * TILE_Y), lambda i, at: (at[1], 0, 0)),
                pl.BlockSpec((None, 2 * KX, 6 * TILE_X), lambda i, at: (at[0], 0, 0)),
            ],
            out_specs=[chunk, whole((4096, 128))],
            scratch_shapes=[
                pltpu.VMEM((2, 2 * KY * TILE_X, 128), F32),
                pltpu.VMEM((4096, 128), F32),
            ],
        ),
        out_shape=[
            jax.ShapeDtypeStruct((rows, ROW), BF16),
            jax.ShapeDtypeStruct((4096, 128), BF16),
        ],
        compiler_params=pltpu.CompilerParams(vmem_limit_bytes=24 * MIB),
        name="project",
    )(place, cotangent, preact, table["project"], table["forward_y"], table["forward_x"])


def update_kernel(sum_ref, spectra_ref, weight_ref, spread_o_ref, spread_c_ref, gw_ref, sg_ref):
    norm = 1.0 / math.sqrt(NX * NY * DEPTH)
    grad = jnp.sum(sum_ref[...], 0) * norm
    saved = jnp.concatenate([spectra_ref[:, b * 128 : (b + 1) * 128] for b in range(4)], 0)
    weight = jnp.concatenate([weight_ref[:, b * 2048 : (b + 1) * 2048] for b in range(4)], 0)
    grad_wide = sum_parts(dot(three_parts(grad), spread_o_ref[...]))
    saved_wide = sum_parts(dot(three_parts(saved), spread_c_ref[...]))

    def combine(value):
        real, imaginary = value[:4], value[4:]
        grad_real, grad_imaginary = grad_wide[:4], grad_wide[4:]
        return jnp.concatenate(
            [
                real * grad_real + imaginary * grad_imaginary,
                real * grad_imaginary - imaginary * grad_real,
            ],
            0,
        )

    outer = combine(saved_wide)
    for b in range(4):
        gw_ref[:, b * 2048 : (b + 1) * 2048] = outer[2 * b : 2 * b + 2]
    back = lax.dot_general(
        three_parts(combine(weight)),
        spread_c_ref[...],
        (((1,), (1,)), ((), ())),
        preferred_element_type=F32,
    )
    back = sum_parts(back)
    sg_ref[...] = jnp.broadcast_to(back[None], sg_ref.shape).astype(sg_ref.dtype)


def update_call(sums, spectra, weight, table):
    return pl.pallas_call(
        update_kernel,
        out_shape=[
            jax.ShapeDtypeStruct((2, 8192), F32),
            jax.ShapeDtypeStruct((ZL * ZH, 8, 128), BF16),
        ],
        compiler_params=pltpu.CompilerParams(vmem_limit_bytes=16 * MIB),
        name="update",
    )(sums, spectra, weight, table["spread_o"], table["spread_c"])


def expand_kernel(
    at_ref,
    modes_ref,
    slope_ref,
    local_ref,
    high_ref,
    low_ref,
    iy_ref,
    ix_ref,
    out_ref,
    m_ref,
    e_refs,
    l_ref,
):
    step = pl.program_id(0)

    @pl.when(step == 0)
    def _():
        m_ref[...] = modes_ref[...].astype(F32)
        for ky in range(KY):
            parts = [
                jnp.concatenate(
                    [m_ref[mode_rows(ky, part * 2 + half), :] for half in range(2)], 1
                )
                for part in range(2)
            ]
            stacked = jnp.concatenate(parts, 0).astype(BF16)
            turned = dot(ix_ref[...], jnp.concatenate([stacked, stacked], 0))
            rows = slice(ky * 2 * TILE_X, (ky + 1) * 2 * TILE_X)
            for half in range(2):
                e_refs[half, rows, :] = turned[:, half * 128 : (half + 1) * 128]
        shape = (16 * CH, CH)
        pick = lax.broadcasted_iota(jnp.int32, shape, 0) % CH
        pick = (pick == lax.broadcasted_iota(jnp.int32, shape, 1)).astype(F32).astype(BF16)
        rows = lax.dot_general(
            pick, local_ref[...], (((1,), (1,)), ((), ())), preferred_element_type=F32
        ).astype(BF16)
        full = lax.dot_general(
            rows, pick, (((1,), (1,)), ((), ())), preferred_element_type=F32
        )
        shape = (16 * CH, 16 * CH)
        same = (
            lax.broadcasted_iota(jnp.int32, shape, 0) // CH
            == lax.broadcasted_iota(jnp.int32, shape, 1) // CH
        )
        l_ref[...] = jnp.where(same, full, 0.0).astype(BF16)

    cells = []
    for local in range(STEP_X):
        at = step * STEP_X + local
        parts = [
            jnp.concatenate(
                [
                    e_refs[half, pl.ds(part * TILE_X + at, KY, stride=2 * TILE_X), :]
                    for half in range(2)
                ],
                1,
            )
            for part in range(2)
        ]
        turned = dot(iy_ref[...], split_rows(jnp.concatenate(parts, 0)))
        cells.append(jnp.concatenate([turned[:TILE_Y], turned[TILE_Y:]], 1))
    high, low = split(jnp.concatenate(cells, 0))
    total = dot(high, high_ref[...]) + dot(low, high_ref[...]) + dot(high, low_ref[...])
    slope = slope_ref[...]
    for part in range(4):
        lanes = slice(part * 256, (part + 1) * 256)
        out_ref[:, lanes] = total[:, lanes] + dot(slope[:, lanes], l_ref[...])


def expand_call(place, modes, slope, local_weight, table):
    def whole(shape):
        return pl.BlockSpec(shape, lambda i, at: (0, 0))

    rows = TILE_X * TILE_Y
    chunk = pl.BlockSpec((STEP_ROWS, ROW), lambda i, at: (i, 0))
    return pl.pallas_call(
        expand_kernel,
        grid_spec=pltpu.PrefetchScalarGridSpec(
            num_scalar_prefetch=1,
            grid=(STEPS,),
            in_specs=[
                whole((4096, 128)),
                chunk,
                whole((CH, CH)),
                whole((2 * HALF, ROW)),
                whole((2 * HALF, ROW)),
                pl.BlockSpec((None, 2 * TILE_Y, 6 * KY), lambda i, at: (at[1], 0, 0)),
                pl.BlockSpec((None, 2 * TILE_X, 4 * KX), lambda i, at: (at[0], 0, 0)),
            ],
            out_specs=chunk,
            scratch_shapes=[
                pltpu.VMEM((4096, 128), F32),
                pltpu.VMEM((2, 2 * KY * TILE_X, 128), F32),
                pltpu.VMEM((16 * CH, 16 * CH), BF16),
            ],
        ),
        out_shape=jax.ShapeDtypeStruct((rows, ROW), F32),
        compiler_params=pltpu.CompilerParams(vmem_limit_bytes=24 * MIB),
        name="expand",
    )(
        place,
        modes,
        slope,
        local_weight,
        table["expand_high"],
        table["expand_low"],
        table["inverse_y"],
        table["inverse_x"],
    )


PLANE = ("y", "x", "c")
LINE = ("zl", "zh")


def on_device(cotangent, preact, spectra, spectral_weight, local_weight):
    table = {name: jnp.asarray(value) for name, value in tables().items()}
    place = jnp.stack([lax.axis_index(("zl", "x", "c")), lax.axis_index(("zh", "y"))])
    place = place.astype(jnp.int32)
    rows = TILE_X * TILE_Y
    slope, partial = project_call(
        place, cotangent.reshape(rows, ROW), preact.reshape(rows, ROW), table
    )
    partial = lax.all_to_all(partial.reshape(32, 128, 128), PLANE, 0, 0, tiled=True)
    sums = jnp.sum(partial.astype(F32), 0).reshape(ZL * ZH, 8, 128)
    sums = lax.all_to_all(sums, LINE, 0, 0, tiled=True)
    grad_weight, back = update_call(
        sums, spectra.reshape(2, 2 * HALF), spectral_weight.reshape(2, 8192), table
    )
    back = lax.all_to_all(back, LINE, 0, 0, tiled=True)
    back = jnp.broadcast_to(back.reshape(1, 128, 128), (32, 128, 128))
    modes = lax.all_to_all(back, PLANE, 0, 0, tiled=True)
    result = expand_call(place, modes.reshape(4096, 128), slope, local_weight, table)
    return result.reshape(TILE_X, TILE_Y, ROW), grad_weight.reshape(1, 2, 8192)


def solution(mesh):
    fine = Mesh(mesh.devices.reshape(ZL, XS, CS, ZH, YS), ("zl", "x", "c", "zh", "y"))
    split_spec = P(("zl", "x", "c"), ("zh", "y"), None)
    return jax.shard_map(
        on_device,
        mesh=fine,
        in_specs=(split_spec, split_spec, split_spec, split_spec, P()),
        out_specs=(split_spec, split_spec),
        check_vma=False,
    )
```

time: 1610 us -> 110 us (0.07)
  waiting for transfers between devices: 1500 us -> 0 us
  blocking collectives: 0 us -> 89.9 us
  matrix products: 50 us -> 0 us
  local copies, waits for them, and re-layouts: 42 us -> 6.04 us
    all_gather x1 -> x0, waiting for transfers between devices: 1020 us -> none  [on_device(): lax.all_gather(spectra_grad.reshape(block_first * block_second, features)...]
    unnamed x3 -> x0, waiting for transfers between devices: 481 us -> none
    all_to_all x0 -> x4, blocking collectives: none -> 89.9 us  [the longest x1 27 us: on_device(): lax.all_to_all(partial.reshape(32, 128, 128), PLANE, 0, 0, tiled=True)]
    dot_general x23 -> x0, matrix products: 50 us -> none  [the longest x16 26.5 us: contract(): return jnp.einsum(form, operand, factor, precision=PRECISE)]
  transfers between devices with their start and end apart: 2 -> 0, of which waited for: 2 -> 0; matrix products, arithmetic and copies ran while one was open for 1% -> 0% of each run, Pallas kernels for 0% -> 0%
where the time goes in v1:
time: 110 us; the launch traced here: 109 us
  blocking collectives  89.9 us (82%)
  Pallas kernels  12.2 us (11%)
  local copies, waits for them, and re-layouts  6.04 us (5%)
    all_to_all x1, blocking collectives, on_device(): lax.all_to_all(partial.reshape(32, 128, 128), PLANE, 0, 0, tiled=True)  27 us
    all_to_all x1, blocking collectives, on_device(): sums = lax.all_to_all(sums, LINE, 0, 0, tiled=True)  25.2 us
    all_to_all x1, blocking collectives, on_device(): modes = lax.all_to_all(back, PLANE, 0, 0, tiled=True)  23.2 us
    all_to_all x1, blocking collectives, on_device(): back = lax.all_to_all(back, LINE, 0, 0, tiled=True)  14.6 us
    pallas_call x1, Pallas kernels, expand_call(): pl.pallas_call(expand_kernel, grid_spec=pltpu.PrefetchScalarGridSpec(num_...  6.68 us
    unnamed x28, local copies, waits for them, and re-layouts  5.82 us
    pallas_call x1, Pallas kernels, project_call(): pl.pallas_call(project_kernel, grid_spec=pltpu.PrefetchScalarGridSpec(num...  4.62 us

profile of v1, /device:TPU:1, one launch (start us, length us, event | category | flops | bytes accessed | tf_op | source)
XLA Modules:
  0.0 109.2 jit_solution(5192964024807108350)
XLA Ops:
  0.6 0.1 pad_add_fusion.at_ref
  0.7 0.0 copy-start
  0.7 1.2 %copy-done = bf16[16,32,1024]{2,1,0:T(8,128)(2,1)S(1)} copy-done((bf16[16,32,1024]{2,1,0:T(8,128)(2,1)S(1)}, bf16[16,32,1024]{2,1,0:T(8,128)(2,1)}, u32[]{:S(2)}) %copy-start) | copy-done | bytes 1048600
  1.9 0.0 copy-start.1
  1.9 1.2 %copy-done.1 = bf16[16,32,1024]{2,1,0:T(8,128)(2,1)S(1)} copy-done((bf16[16,32,1024]{2,1,0:T(8,128)(2,1)S(1)}, bf16[16,32,1024]{2,1,0:T(8,128)(2,1)}, u32[]{:S(2)}) %copy-start.1) | copy-done | bytes 1048600
  3.2 0.0 copy-start.4
  3.2 1.2 %copy-done.4 = bf16[1024,512]{1,0:T(8,128)(2,1)S(1)} copy-done((bf16[1024,512]{1,0:T(8,128)(2,1)S(1)}, bf16[1024,512]{1,0:T(8,128)(2,1)}, u32[]{:S(2)}) %copy-start.4) | copy-done | bytes 1048600
  4.4 0.0 copy-start.6
  4.4 1.0 copy-done.6
  5.4 0.0 copy-start.7
  5.4 1.0 copy-done.7
  6.5 4.6 %project.1 = (bf16[512,1024]{1,0:T(8,128)(2,1)S(1)}, bf16[4096,128]{1,0:T(8,128)(2,1)S(1)}) custom-call(s32[2]{0:T(128)S(1)} %pad_add_fusion.at_ref, bf16[512,1024]{1,0:T(8,128)(2,1)S(1)} %bitcast.13, bf16[512,1024]{1,0:T(8,128)(2,1)S(1)} %bitcast.14, bf16[1024,512]{1,0:T(8,128)(2,1)S(1)} %copy-done.4, bf16[16,64,192]{2,1,0:T(8,128)(2,1)S(1)} %copy-done.7, ...), custom_call_target="tpu_custom_call" | custom-call | tf_op jit(solution)/shard_map/project/pallas_call | solution.py:180
  11.1 0.0 copy-start.8
  11.1 0.0 copy-start.9
  11.1 0.0 copy-start.11
  11.1 0.0 copy-start.12
  11.2 27.0 %all_to_all.20 = bf16[32,128,128]{2,1,0:T(8,128)(2,1)S(1)} all-to-all(bf16[32,128,128]{2,1,0:T(8,128)(2,1)S(1)} %bitcast.15), channel_id=1, replica_groups=mesh['zl'=4,'x'=4,'c'=2,'zh'=4,'y'=4] {'y','x','c'}, dimensions={0} | all-to-all | bytes 2097152 | tf_op jit(solution)/shard_map/all_to_all | solution.py:375
  38.1 0.2 convert_reduce_fusion
  38.3 25.2 %all_to_all.21.sum_ref = f32[16,8,128]{2,1,0:T(8,128)S(1)} all-to-all(f32[16,8,128]{2,1,0:T(8,128)S(1)} %bitcast.19), channel_id=1, replica_groups=mesh['zl'=4,'x'=4,'c'=2,'zh'=4,'y'=4] {'zl','zh'}, dimensions={0} | all-to-all | bytes 131072 | tf_op jit(solution)/shard_map/all_to_all | solution.py:377
  63.5 0.0 copy-done.8
  63.5 0.0 copy-done.9
  63.5 0.0 copy-done.11
  63.5 0.0 copy-done.12
  63.5 0.0 copy-start.2
  63.5 0.0 copy-start.3
  63.5 0.0 copy-start.5
  63.5 0.0 copy-start.10
  63.5 0.0 copy-start.13
  63.6 0.9 update.1
  64.5 14.6 %all_to_all.22 = bf16[16,8,128]{2,1,0:T(8,128)(2,1)S(1)} all-to-all(bf16[16,8,128]{2,1,0:T(8,128)(2,1)S(1)} %get-tuple-element.7), channel_id=1, replica_groups=mesh['zl'=4,'x'=4,'c'=2,'zh'=4,'y'=4] {'zl','zh'}, dimensions={0} | all-to-all | bytes 65536 | tf_op jit(solution)/shard_map/all_to_all | solution.py:381
  79.1 0.2 broadcast_in_dim.8
  79.3 23.2 %all_to_all.23 = bf16[32,128,128]{2,1,0:T(8,128)(2,1)S(1)} all-to-all(bf16[32,128,128]{2,1,0:T(8,128)(2,1)S(1)} %broadcast_in_dim.8), channel_id=1, replica_groups=mesh['zl'=4,'x'=4,'c'=2,'zh'=4,'y'=4] {'y','x','c'}, dimensions={0} | all-to-all | bytes 2097152 | tf_op jit(solution)/shard_map/all_to_all | solution.py:383
  102.5 0.0 copy-done.2
  102.5 0.0 copy-done.3
  102.5 0.0 copy-done.5
  102.5 0.0 copy-done.10
  102.5 0.0 copy-done.13
  102.5 6.7 %expand.1 = f32[512,1024]{1,0:T(8,128)} custom-call(s32[2]{0:T(128)S(1)} %pad_add_fusion.at_ref, bf16[4096,128]{1,0:T(8,128)(2,1)S(1)} %bitcast.12, bf16[512,1024]{1,0:T(8,128)(2,1)S(1)} %get-tuple-element.8.slope_ref, bf16[16,16]{1,0:T(8,128)(2,1)S(1)} %copy-done.13, bf16[512,1024]{1,0:T(8,128)(2,1)S(1)} %copy-done.3, bf16[512,1024]{1,0:T(8,128)(2,1)S(1)} %copy-done.2, ...), custom_call_target="tpu_custom_call" | custom-call | tf_op jit(solution)/shard_map/expand/pallas_call | solution.py:327
Async XLA Ops:
  0.7 1.2 %copy-start = (bf16[16,32,1024]{2,1,0:T(8,128)(2,1)S(1)}, bf16[16,32,1024]{2,1,0:T(8,128)(2,1)}, u32[]{:S(2)}) copy-start(bf16[16,32,1024]{2,1,0:T(8,128)(2,1)} %param.14) | copy-start | bytes 3145732
  1.9 1.2 %copy-start.1 = (bf16[16,32,1024]{2,1,0:T(8,128)(2,1)S(1)}, bf16[16,32,1024]{2,1,0:T(8,128)(2,1)}, u32[]{:S(2)}) copy-start(bf16[16,32,1024]{2,1,0:T(8,128)(2,1)} %param.15) | copy-start | bytes 3145732
  3.2 1.2 %copy-start.4 = (bf16[1024,512]{1,0:T(8,128)(2,1)S(1)}, bf16[1024,512]{1,0:T(8,128)(2,1)}, u32[]{:S(2)}) copy-start(bf16[1024,512]{1,0:T(8,128)(2,1)} %constant.51.clone.project_ref) | copy-start | bytes 3145732
  4.4 1.0 copy-start.6
  5.4 1.0 copy-start.7
  11.1 52.4 %copy-start.8 = (bf16[128,2048]{1,0:T(8,128)(2,1)S(1)}, bf16[128,2048]{1,0:T(8,128)(2,1)}, u32[]{:S(2)}) copy-start(bf16[128,2048]{1,0:T(8,128)(2,1)} %constant.55.clone.spread_c_ref) | copy-start | bytes 1572868
  11.1 52.4 %copy-start.9 = (bf16[128,2048]{1,0:T(8,128)(2,1)S(1)}, bf16[128,2048]{1,0:T(8,128)(2,1)}, u32[]{:S(2)}) copy-start(bf16[128,2048]{1,0:T(8,128)(2,1)} %constant.54.clone.spread_o_ref) | copy-start | bytes 1572868
  11.1 52.4 %copy-start.11 = (f32[1,2,8192]{2,1,0:T(2,128)S(1)}, f32[1,2,8192]{2,1,0:T(2,128)}, u32[]{:S(2)}) copy-start(f32[1,2,8192]{2,1,0:T(2,128)} %param.17) | copy-start | bytes 196612
  11.1 52.4 %copy-start.12 = (f32[1,2,512]{2,1,0:T(2,128)S(1)}, f32[1,2,512]{2,1,0:T(2,128)}, u32[]{:S(2)}) copy-start(f32[1,2,512]{2,1,0:T(2,128)} %param.16) | copy-start | bytes 12292
  63.5 39.0 %copy-start.2 = (bf16[512,1024]{1,0:T(8,128)(2,1)S(1)}, bf16[512,1024]{1,0:T(8,128)(2,1)}, u32[]{:S(2)}) copy-start(bf16[512,1024]{1,0:T(8,128)(2,1)} %constant.53.clone.low_ref) | copy-start | bytes 3145732
  63.5 39.0 %copy-start.3 = (bf16[512,1024]{1,0:T(8,128)(2,1)S(1)}, bf16[512,1024]{1,0:T(8,128)(2,1)}, u32[]{:S(2)}) copy-start(bf16[512,1024]{1,0:T(8,128)(2,1)} %constant.52.clone.high_ref) | copy-start | bytes 3145732
  63.5 39.0 %copy-start.5 = (bf16[16,64,192]{2,1,0:T(8,128)(2,1)S(1)}, bf16[16,64,192]{2,1,0:T(8,128)(2,1)}, u32[]{:S(2)}) copy-start(bf16[16,64,192]{2,1,0:T(8,128)(2,1)} %constant.48.clone.iy_ref) | copy-start | bytes 1179652
  63.5 39.0 %copy-start.10 = (bf16[32,32,128]{2,1,0:T(8,128)(2,1)S(1)}, bf16[32,32,128]{2,1,0:T(8,128)(2,1)}, u32[]{:S(2)}) copy-start(bf16[32,32,128]{2,1,0:T(8,128)(2,1)} %constant.50.clone.ix_ref) | copy-start | bytes 786436
  63.5 39.0 %copy-start.13 = (bf16[16,16]{1,0:T(8,128)(2,1)S(1)}, bf16[16,16]{1,0:T(8,128)(2,1)}, u32[]{:S(2)}) copy-start(bf16[16,16]{1,0:T(8,128)(2,1)} %local_ref.1) | copy-start | bytes 1540

commit v2 on v1

v2 whole, which is shorter than its diff:
```python
import functools
import math

import jax
import jax.numpy as jnp
import ml_dtypes
import numpy as np
from jax import lax
from jax.experimental import pallas as pl
from jax.experimental.pallas import tpu as pltpu
from jax.sharding import Mesh
from jax.sharding import PartitionSpec as P

TILE_X, TILE_Y, DEPTH, CH = 16, 32, 64, 16
KX, KY, KZ = 32, 32, 16
NX, NY = 512, 512
ZL, XS, CS, ZH, YS = 4, 4, 2, 4, 4
ROW = DEPTH * CH
HALF = KZ * CH
QUARTER = 128
ROWS = TILE_X * TILE_Y
CHUNKS = 8
CHUNK_ROWS = ROWS // CHUNKS
NORM = 1.0 / math.sqrt(NX * NY * DEPTH)
F32, BF16 = jnp.float32, jnp.bfloat16
MIB = 1024 * 1024
PLANE = ("y", "x")
LINE = ("zl", "zh", "c")


def split_table(table):
    high = table.astype(ml_dtypes.bfloat16)
    low = (table - high.astype(np.float64)).astype(ml_dtypes.bfloat16)
    return high, low


def mode_ids(count, length):
    ordinal = np.arange(count)
    return np.where(ordinal < count // 2, ordinal, ordinal + length - count)


def phase(positions, modes, length):
    angle = (np.outer(modes, positions) % length) * (2.0 * np.pi / length)
    return np.cos(angle), np.sin(angle)


KX_ORDER = np.array([zl * 8 + x * 2 + c for x in range(XS) for zl in range(ZL) for c in range(CS)])
KY_ORDER = np.array([zh * 8 + y * 2 + k for y in range(YS) for zh in range(ZH) for k in range(2)])


def rotation(cosine, sine):
    return np.stack([np.stack([cosine, sine]), np.stack([-sine, cosine])])


@functools.cache
def tables():
    ky = mode_ids(KY, NY)[KY_ORDER]
    kx = mode_ids(KX, NX)[KX_ORDER]
    forward_y, inverse_y, forward_x = [], [], []
    for tile in range(NY // TILE_Y):
        turn = rotation(*phase(tile * TILE_Y + np.arange(TILE_Y), ky, NY))
        turn = turn.reshape(2, 2, YS, 8, TILE_Y)
        rows = turn.transpose(2, 0, 3, 1, 4).reshape(2 * KY, 2 * TILE_Y)
        high, low = split_table(rows)
        forward_y.append(np.concatenate([high, high, low], 1))
        high, low = split_table(rows.reshape(2 * KY, 2, TILE_Y).transpose(1, 2, 0).reshape(2 * TILE_Y, -1))
        inverse_y.append(np.concatenate([high, high, low], 1))
    for tile in range(NX // TILE_X):
        parts = []
        for source in (tile, tile ^ 1):
            turn = rotation(*phase(source * TILE_X + np.arange(TILE_X), kx, NX))
            parts.append(turn.transpose(2, 0, 3, 1).reshape(2 * KX, 2 * TILE_X))
        forward_x.append(np.concatenate(split_table(np.concatenate(parts, 1)), 1))
    depth_angle = (np.outer(np.arange(DEPTH), np.arange(KZ)) % DEPTH) * (2.0 * np.pi / DEPTH)
    weight = np.where(np.arange(KZ) == 0, 1.0, 2.0)
    factor = np.stack([np.cos(depth_angle) * weight, -np.sin(depth_angle) * weight], 1)
    factor = factor.astype(np.float32).astype(ml_dtypes.bfloat16).astype(np.float32)
    project = np.repeat(factor.reshape(DEPTH, 2, 2, 8).transpose(2, 0, 1, 3), CH, 3)
    project = project.reshape(2, DEPTH, HALF).astype(ml_dtypes.bfloat16)
    expand = np.stack([np.cos(depth_angle).T, -np.sin(depth_angle).T], 0) * NORM
    expand = expand.reshape(2, 2, 8, DEPTH).transpose(1, 0, 2, 3).reshape(2, KZ, DEPTH)
    expand = np.stack([np.kron(part, np.eye(CH)) for part in expand])
    expand_high, expand_low = split_table(expand)
    eye, kz8, ones = np.eye(CH), np.eye(8), np.ones((1, CH))
    spread_o = np.kron(kz8, np.kron(ones, eye)).astype(ml_dtypes.bfloat16)
    spread_c = np.kron(kz8, np.kron(eye, ones)).astype(ml_dtypes.bfloat16)
    return dict(
        forward_y=np.stack(forward_y),
        inverse_y=np.stack(inverse_y),
        forward_x=np.stack(forward_x),
        project=project,
        expand_high=expand_high,
        expand_low=expand_low,
        spread_o=spread_o,
        spread_c=spread_c,
    )


def dot(left, right):
    return lax.dot_general(left, right, (((1,), (0,)), ((), ())), preferred_element_type=F32)


def dot_last(left, right):
    return lax.dot_general(left, right, (((1,), (1,)), ((), ())), preferred_element_type=F32)


def split(value):
    high = value.astype(BF16)
    return high, (value - high.astype(F32)).astype(BF16)


def store_split(ref, lanes, value):
    rows = value.shape[0]
    high, low = split(value)
    ref[:rows, lanes] = high
    ref[rows : 2 * rows, lanes] = low
    ref[2 * rows :, lanes] = high


def three_parts(value):
    high = value.astype(BF16)
    rest = value - high.astype(F32)
    middle = rest.astype(BF16)
    low = (rest - middle.astype(F32)).astype(BF16)
    return jnp.concatenate([high, middle, low], 0)


def sum_parts(value):
    rows = value.shape[0] // 3
    return value[:rows] + (value[rows : 2 * rows] + value[2 * rows :])


def gelu_slope(pre_value):
    normal_cdf = 0.5 * (1.0 + lax.erf(pre_value * (1.0 / math.sqrt(2.0))))
    return normal_cdf + pre_value * jnp.exp(-0.5 * pre_value * pre_value) * (
        1.0 / math.sqrt(2.0 * math.pi)
    )


def lanes_of(at):
    return slice(at * QUARTER, (at + 1) * QUARTER)


def iota(shape, axis):
    return lax.broadcasted_iota(jnp.int32, shape, axis)


def one_hot(condition):
    return condition.astype(F32).astype(BF16)


BLOCK, CELLS = 512, 256


def fill_forward(out_ref, small):
    shape = (128, 1024)
    cells = one_hot(iota(shape, 1) >> 3 == iota(shape, 0))
    shape = (128, 64)
    twice = one_hot(iota(shape, 0) >> 1 == iota(shape, 1))
    wide = dot(twice, dot(small, cells).astype(BF16))
    shape = (8, CELLS)
    local, ky = iota(shape, 0) & 1, iota(shape, 1) & 7
    masks = [(ky == 2 * zh + local).astype(F32) for zh in range(ZH)]
    for part in range(2):
        for source in range(2):
            first = (part * 2 + source) * CELLS
            for group in range(16):
                rows = wide[group * 8 : (group + 1) * 8, first : first + CELLS]
                rows = jnp.concatenate([rows * mask for mask in masks], 0).astype(BF16)
                out_ref[source, part, group * 32 : (group + 1) * 32, :] = rows


def fill_inverse(out_ref, small):
    shape = (64, BLOCK)
    row, column = iota(shape, 0), iota(shape, 1)
    modes = one_hot((column >> 5) * 4 + (column >> 1 & 3) == row)
    wide = lax.dot_general(small, modes, (((0,), (0,)), ((), ())), preferred_element_type=F32)
    shape = (8, BLOCK)
    row, column = iota(shape, 0), iota(shape, 1)
    mask = ((column >> 3 & 3) * 2 + (column & 1) == row).astype(F32)
    for part in range(2):
        for cell in range(TILE_X):
            at = part * 64 + cell * 2
            rows = [jnp.broadcast_to(wide[i : i + 1], shape) * mask for i in (at, at + 1)]
            out_ref[part, cell * 16 : (cell + 1) * 16, :] = jnp.concatenate(rows, 0).astype(BF16)


def fill_local(out_ref, local_ref):
    shape = (16 * CH, CH)
    pick = one_hot((iota(shape, 0) & (CH - 1)) == iota(shape, 1))
    full = dot_last(dot_last(pick, local_ref[...]).astype(BF16), pick)
    shape = (16 * CH, 16 * CH)
    same = iota(shape, 0) >> 4 == iota(shape, 1) >> 4
    out_ref[...] = jnp.where(same, full, 0.0).astype(BF16)


def fill_project(f_ref, table_ref, half):
    shape = (CH, HALF)
    same = iota(shape, 0) == (iota(shape, 1) & (CH - 1))
    table = table_ref[half].astype(F32)
    for z in range(DEPTH):
        factor = jnp.broadcast_to(table[z : z + 1], shape)
        f_ref[z * CH : (z + 1) * CH, :] = jnp.where(same, factor, 0.0).astype(BF16)


def slope_kernel(
    at_ref,
    cot_hbm,
    pre_hbm,
    local_hbm,
    table_hbm,
    fx_hbm,
    fy_hbm,
    iy_hbm,
    slope_ref,
    send_ref,
    own_ref,
    forward_ref,
    inverse_ref,
    l_ref,
    fy_ref,
    iy_ref,
    cot_ref,
    pre_ref,
    local_ref,
    table_ref,
    fx_ref,
    f_ref,
    sems,
    small_sems,
):
    def copies(chunk):
        rows = pl.ds(chunk * CHUNK_ROWS, CHUNK_ROWS)
        return (
            pltpu.make_async_copy(cot_hbm.at[rows], cot_ref.at[rows], sems.at[0, chunk]),
            pltpu.make_async_copy(pre_hbm.at[rows], pre_ref.at[rows], sems.at[1, chunk]),
        )

    small = [
        pltpu.make_async_copy(source, target, small_sems.at[i])
        for i, (source, target) in enumerate(
            (
                (fx_hbm.at[at_ref[0]], fx_ref),
                (table_hbm, table_ref),
                (local_hbm, local_ref),
                (fy_hbm.at[at_ref[1]], fy_ref),
                (iy_hbm.at[at_ref[1]], iy_ref),
            )
        )
    ]
    for copy in small:
        copy.start()
    for chunk in range(CHUNKS):
        for copy in copies(chunk):
            copy.start()
    for copy in small:
        copy.wait()
    fill_project(f_ref, table_ref, 1 - at_ref[2])
    fill_project(own_ref, table_ref, at_ref[2])
    fill_forward(forward_ref, fx_ref[...])
    fill_inverse(inverse_ref, fx_ref[...])
    fill_local(l_ref, local_ref)
    for chunk in range(CHUNKS):
        for copy in copies(chunk):
            copy.wait()
        rows = slice(chunk * CHUNK_ROWS, (chunk + 1) * CHUNK_ROWS)
        pre_value = pre_ref[rows, :].astype(F32)
        slope = (cot_ref[rows, :].astype(F32) * gelu_slope(pre_value)).astype(BF16)
        slope_ref[rows, :] = slope
        if (chunk + 1) * 2 % CHUNKS == 0:
            rows = slice((chunk + 1) * CHUNK_ROWS - ROWS // 2, (chunk + 1) * CHUNK_ROWS)
            send_ref[rows, :] = dot(slope_ref[rows, :], f_ref[...])


def turn_y(depth, fy_ref, rhs_ref, high_ref, low_ref):
    for x in range(TILE_X):
        block = depth[x * TILE_Y : (x + 1) * TILE_Y]
        stacked = jnp.concatenate([block[:, :QUARTER], block[:, QUARTER:]], 0)
        store_split(rhs_ref, lanes_of(x), stacked)
    turned = dot(fy_ref[...], rhs_ref[...])
    for x in range(TILE_X):
        for y in range(YS):
            high, low = split(turned[y * 16 : (y + 1) * 16, lanes_of(x)])
            high_ref[x * 16 : (x + 1) * 16, lanes_of(y)] = high
            low_ref[x * 16 : (x + 1) * 16, lanes_of(y)] = low


def turn_x(table_high, table_low, high, low):
    return dot(table_high, high) + dot(table_high, low) + dot(table_low, high)


def own_kernel(slope_ref, f_ref, x_ref, fy_ref, part_ref, rhs_ref, high_ref, low_ref):
    turn_y(dot(slope_ref[...], f_ref[...]), fy_ref, rhs_ref, high_ref, low_ref)
    part_ref[...] = turn_x(x_ref[0, 0], x_ref[0, 1], high_ref[...], low_ref[...])


def modes_kernel(depth_ref, part_ref, x_ref, fy_ref, out_ref, rhs_ref, high_ref, low_ref):
    turn_y(depth_ref[...], fy_ref, rhs_ref, high_ref, low_ref)
    turned = part_ref[...] + turn_x(x_ref[1, 0], x_ref[1, 1], high_ref[...], low_ref[...])
    for y in range(YS):
        out_ref[y * BLOCK : (y + 1) * BLOCK, :] = turned[:, lanes_of(y)].astype(BF16)


def update_kernel(
    sum_ref, spectra_ref, weight_ref, spread_o_ref, spread_c_ref, gw_ref, sg_ref
):
    halves = [jnp.sum(sum_ref[:, half], 0) * NORM for half in range(2)]
    grad = jnp.concatenate([halves[0][:2], halves[1][:2], halves[0][2:], halves[1][2:]], 0)
    saved = jnp.concatenate([spectra_ref[:, b * 128 : (b + 1) * 128] for b in range(4)], 0)
    weight = jnp.concatenate([weight_ref[:, b * 2048 : (b + 1) * 2048] for b in range(4)], 0)
    grad_wide = sum_parts(dot(three_parts(grad), spread_o_ref[...]))
    saved_wide = sum_parts(dot(three_parts(saved), spread_c_ref[...]))

    def combine(value):
        real, imaginary = value[:4], value[4:]
        grad_real, grad_imaginary = grad_wide[:4], grad_wide[4:]
        return jnp.concatenate(
            [
                real * grad_real + imaginary * grad_imaginary,
                real * grad_imaginary - imaginary * grad_real,
            ],
            0,
        )

    outer = combine(saved_wide)
    for b in range(4):
        gw_ref[:, b * 2048 : (b + 1) * 2048] = outer[2 * b : 2 * b + 2]
    back = sum_parts(dot_last(three_parts(combine(weight)), spread_c_ref[...]))
    back = back.astype(BF16).astype(F32)
    for half in range(2):
        rows = jnp.concatenate([back[2 * half : 2 * half + 2], back[2 * half + 4 : 2 * half + 6]], 0)
        sg_ref[:, half] = jnp.broadcast_to(rows[None], (ZL * ZH, 4, QUARTER))


def turn_back(modes_ref, table_high, table_low, iy_ref, wide_ref, rhs_ref):
    for y in range(YS):
        wide_ref[:, lanes_of(y)] = modes_ref[y * BLOCK : (y + 1) * BLOCK, :]
    turned = dot(table_high, wide_ref[...]) + dot(table_low, wide_ref[...])
    for x in range(TILE_X):
        for y in range(YS):
            high, low = split(turned[x * 16 : (x + 1) * 16, lanes_of(y)])
            for at, part in enumerate((high, low, high)):
                rows = slice(at * 2 * KY + y * 16, at * 2 * KY + (y + 1) * 16)
                rhs_ref[rows, lanes_of(x)] = part
    turned = dot(iy_ref[...], rhs_ref[...])
    cells = [
        jnp.concatenate([turned[:TILE_Y, lanes_of(x)], turned[TILE_Y:, lanes_of(x)]], 1)
        for x in range(TILE_X)
    ]
    return jnp.concatenate(cells, 0)


def expand_own_kernel(
    at_ref,
    modes_ref,
    slope_ref,
    l_ref,
    high_ref,
    low_ref,
    x_ref,
    iy_ref,
    out_ref,
    wide_ref,
    rhs_ref,
):
    cells = turn_back(modes_ref, x_ref[0], x_ref[1], iy_ref, wide_ref, rhs_ref)
    high, low = split(cells)
    half = at_ref[2]
    for part in range(4):
        lanes = slice(part * 256, (part + 1) * 256)
        table = high_ref[half, :, lanes]
        out_ref[:, lanes] = (
            dot(high, table)
            + dot(low, table)
            + dot(high, low_ref[half, :, lanes])
            + dot(slope_ref[:, lanes], l_ref[...])
        )


def expand_kernel(
    at_ref,
    modes_ref,
    part_ref,
    high_ref,
    low_ref,
    x_ref,
    iy_ref,
    out_hbm,
    wide_ref,
    rhs_ref,
    out_ref,
    sems,
):
    cells = turn_back(modes_ref, x_ref[0], x_ref[1], iy_ref, wide_ref, rhs_ref)
    high, low = split(cells)
    half = 1 - at_ref[2]
    copies = []
    for part in range(4):
        lanes = slice(part * 256, (part + 1) * 256)
        table = high_ref[half, :, lanes]
        out_ref[:, lanes] = (
            dot(high, table)
            + dot(low, table)
            + dot(high, low_ref[half, :, lanes])
            + part_ref[:, lanes]
        )
        copies.append(
            pltpu.make_async_copy(out_ref.at[:, lanes], out_hbm.at[:, lanes], sems.at[part])
        )
        copies[-1].start()
    for copy in copies:
        copy.wait()


def in_vmem(count):
    return [pl.BlockSpec(memory_space=pltpu.VMEM)] * count


SMEM = pl.BlockSpec(memory_space=pltpu.SMEM)
IN_HBM = pl.BlockSpec(memory_space=pltpu.HBM)


def call(kernel, name, outs, ins, out_specs, scratch, flops=0):
    return pl.pallas_call(
        kernel,
        in_specs=ins,
        out_specs=out_specs,
        out_shape=[jax.ShapeDtypeStruct(*out) for out in outs],
        scratch_shapes=scratch,
        compiler_params=pltpu.CompilerParams(vmem_limit_bytes=20 * MIB),
        cost_estimate=pl.CostEstimate(flops=flops, bytes_accessed=4 * MIB, transcendentals=0),
        name=name,
    )


def in_hbm(value):
    return pltpu.with_memory_space_constraint(value, pltpu.HBM)


def on_device(cotangent, preact, spectra, spectral_weight, local_weight):
    table = {name: jnp.asarray(value) for name, value in tables().items()}
    place = jnp.stack(
        [lax.axis_index(("zl", "x", "c")), lax.axis_index(("zh", "y")), lax.axis_index("c")]
    ).astype(jnp.int32)
    swap = [(0, 1), (1, 0)]
    square = (ROWS, HALF)
    turn_scratch = pltpu.VMEM((6 * TILE_Y, TILE_X * QUARTER), BF16)
    cell_scratch = [pltpu.VMEM((CELLS, YS * QUARTER), BF16)] * 2

    slope, send, own_project, forward_x, inverse_x, local_map, forward_y, inverse_y = call(
        slope_kernel,
        "slope",
        [
            ((ROWS, ROW), BF16),
            (square, F32),
            ((ROW, HALF), BF16),
            ((2, 2, BLOCK, CELLS), BF16),
            ((2, CELLS, BLOCK), BF16),
            ((16 * CH, 16 * CH), BF16),
            ((2 * KY, 6 * TILE_Y), BF16),
            ((2 * TILE_Y, 6 * KY), BF16),
        ],
        [SMEM, *[IN_HBM] * 7],
        in_vmem(8),
        [
            pltpu.VMEM((ROWS, ROW), BF16),
            pltpu.VMEM((ROWS, ROW), BF16),
            pltpu.VMEM((CH, CH), BF16),
            pltpu.VMEM((2, DEPTH, HALF), BF16),
            pltpu.VMEM((2 * KX, 8 * TILE_X), BF16),
            pltpu.VMEM((ROW, HALF), BF16),
            pltpu.SemaphoreType.DMA((2, CHUNKS)),
            pltpu.SemaphoreType.DMA((5,)),
        ],
    )(
        place,
        in_hbm(cotangent.reshape(ROWS, ROW)),
        in_hbm(preact.reshape(ROWS, ROW)),
        in_hbm(local_weight),
        in_hbm(table["project"]),
        in_hbm(table["forward_x"]),
        in_hbm(table["forward_y"]),
        in_hbm(table["inverse_y"]),
    )
    depth = lax.ppermute(send, "c", swap)
    (own,) = call(
        own_kernel,
        "own_cells",
        [((BLOCK, YS * QUARTER), F32)],
        in_vmem(4),
        in_vmem(1),
        [turn_scratch, *cell_scratch],
        flops=2 * 10**9,
    )(slope, own_project, forward_x, forward_y)
    (partial,) = call(
        modes_kernel,
        "modes",
        [((2048, QUARTER), BF16)],
        in_vmem(4),
        in_vmem(1),
        [turn_scratch, *cell_scratch],
    )(depth, own, forward_x, forward_y)
    partial = lax.all_to_all(partial.reshape(16, 128, QUARTER), PLANE, 0, 0, tiled=True)
    sums = jnp.sum(partial.astype(F32), 0).reshape(32, 4, QUARTER)
    sums = lax.all_to_all(sums, LINE, 0, 0, tiled=True)
    grad_weight, back = call(
        update_kernel,
        "update",
        [((2, 8192), F32), ((ZL * ZH, CS, 4, QUARTER), F32)],
        in_vmem(5),
        in_vmem(2),
        [],
    )(
        sums.reshape(ZL * ZH, CS, 4, QUARTER),
        spectra.reshape(2, 2 * HALF),
        spectral_weight.reshape(2, 8192),
        table["spread_o"],
        table["spread_c"],
    )
    back = lax.all_to_all(back.reshape(32, 4, QUARTER).astype(BF16), LINE, 0, 0, tiled=True)
    back = jnp.broadcast_to(back.reshape(1, 128, QUARTER), (16, 128, QUARTER))
    modes = lax.all_to_all(back, PLANE, 0, 0, tiled=True).reshape(2048, QUARTER)
    other = lax.ppermute(modes, "c", swap)
    back_scratch = [pltpu.VMEM((BLOCK, YS * QUARTER), BF16), turn_scratch]
    depth_tables = (table["expand_high"], table["expand_low"])
    (part,) = call(
        expand_own_kernel,
        "expand_own",
        [((ROWS, ROW), F32)],
        [SMEM, *in_vmem(7)],
        in_vmem(1),
        back_scratch,
        flops=3 * 10**9,
    )(place, modes, slope, local_map, *depth_tables, inverse_x, inverse_y)
    (result,) = call(
        expand_kernel,
        "expand",
        [((ROWS, ROW), F32)],
        [SMEM, *in_vmem(6)],
        [IN_HBM],
        [*back_scratch, pltpu.VMEM((ROWS, ROW), F32), pltpu.SemaphoreType.DMA((4,))],
    )(place, other, part, *depth_tables, inverse_x, inverse_y)
    return result.reshape(TILE_X, TILE_Y, ROW), grad_weight.reshape(1, 2, 8192)


def solution(mesh):
    fine = Mesh(mesh.devices.reshape(ZL, XS, CS, ZH, YS), ("zl", "x", "c", "zh", "y"))
    split_spec = P(("zl", "x", "c"), ("zh", "y"), None)
    return jax.shard_map(
        on_device,
        mesh=fine,
        in_specs=(split_spec, split_spec, split_spec, split_spec, P()),
        out_specs=(split_spec, split_spec),
        check_vma=False,
    )
```

time: 110 us -> 98.3 us (0.89)
  blocking collectives: 89.9 us -> 70.1 us
  starting transfers between devices: 0 us -> 12.8 us
  local copies, waits for them, and re-layouts: 6.04 us -> 0.13 us
  Pallas kernels: 12.2 us -> 14 us
    all_to_all x3, blocking collectives: 64.7 us -> 43.4 us  [the longest x1 16.5 us: on_device(): lax.all_to_all(back.reshape(32, 4, QUARTER).astype(BF16), LINE, 0, 0, til...]
    ppermute x0 -> x2, starting transfers between devices: none -> 12.8 us  [the longest x1 8.78 us: on_device(): depth = lax.ppermute(send, 'c', swap)]
    unnamed x28 -> x12, local copies, waits for them, and re-layouts: 5.82 us -> 0.03 us
    pallas_call x3 -> x6, Pallas kernels: 12.2 us -> 14 us  [the longest x1 4.59 us: on_device(): call(slope_kernel, 'slope', [((ROWS, ROW), BF16), (square, F32), ((ROW, H...]
    all_to_all x1, blocking collectives: 25.2 us -> 26.7 us  [on_device(): sums = lax.all_to_all(sums, LINE, 0, 0, tiled=True)]
  transfers between devices with their start and end apart: 0 -> 2, of which waited for: 0 -> 0; matrix products, arithmetic and copies ran while one was open for 0% -> 0% of each run, Pallas kernels for 0% -> 4%
where the time goes in v2:
time: 98.3 us; the launch traced here: 98 us
  blocking collectives  70.1 us (71%)
  Pallas kernels  14 us (14%)
  starting transfers between devices  12.8 us (13%)
    all_to_all x1, blocking collectives, on_device(): sums = lax.all_to_all(sums, LINE, 0, 0, tiled=True)  26.7 us
    all_to_all x1, blocking collectives, on_device(): lax.all_to_all(back.reshape(32, 4, QUARTER).astype(BF16), LINE, 0, 0, til...  16.5 us
    all_to_all x1, blocking collectives, on_device(): lax.all_to_all(partial.reshape(16, 128, QUARTER), PLANE, 0, 0, tiled=True)  14 us
    all_to_all x1, blocking collectives, on_device(): modes = lax.all_to_all(back, PLANE, 0, 0, tiled=True).reshape(2048, QUARTER)  12.9 us
    ppermute x1, starting transfers between devices, on_device(): depth = lax.ppermute(send, 'c', swap)  8.78 us
    pallas_call x1, Pallas kernels, on_device(): call(slope_kernel, 'slope', [((ROWS, ROW), BF16), (square, F32), ((ROW, H...  4.59 us
    ppermute x1, starting transfers between devices, on_device(): other = lax.ppermute(modes, 'c', swap)  4.06 us
    pallas_call x1, Pallas kernels, on_device(): call(expand_kernel, 'expand', [((ROWS, ROW), F32)], [SMEM, *in_vmem(6)],...  3.3 us
  transfers between devices with their start and end apart: 2, of which 0 were waited for; matrix products, arithmetic and copies ran while one was open for 0% of the time, Pallas kernels for 4%

profile of v2, /device:TPU:1, one launch (start us, length us, event | category | flops | bytes accessed | tf_op | source)
XLA Modules:
  0.0 98.0 jit_solution(1981753564798991588)
XLA Ops:
  0.6 0.1 pad_add_fusion.at_ref
  0.7 4.6 %slope.1 = (bf16[512,1024]{1,0:T(8,128)(2,1)S(1)}, f32[512,256]{1,0:T(8,128)S(1)}, bf16[1024,256]{1,0:T(8,128)(2,1)S(1)}, bf16[2,2,512,256]{3,2,1,0:T(8,128)(2,1...) custom-call(s32[3]{0:T(128)S(1)} %pad_add_fusion.at_ref, ...), custom_call_target="tpu_custom_call" | custom-call | bytes 4194304 | tf_op jit(solution)/shard_map/slope/pallas_call | solution.py:450
  5.3 8.8 %collective-permute-start = (f32[512,256]{1,0:T(8,128)S(1)}, f32[512,256]{1,0:T(8,128)S(1)}, u32[]{:S(2)}, u32[]{:S(2)}) collective-permute-start(f32[512,256]{1,0:T(8,128)S(1)} %get-tuple-element.12), channel_id=1, source_target_pairs={{0,16},{16,0},{1,17},{17,1},{2,18},{18,2},{3,19},{19,3},{4,20},{20... | collective-permute-start | bytes 1572872 | tf_op jit(solution)/shard_map/ppermute | solution.py:485
  14.1 1.7 %own_cells.1.part_ref = f32[512,512]{1,0:T(8,128)S(1)} custom-call(bf16[512,1024]{1,0:T(8,128)(2,1)S(1)} %get-tuple-element.13.slope_ref, bf16[1024,256]{1,0:T(8,128)(2,1)S(1)} %get-tuple-element.14.f_ref, bf16[2,2,512,256]{3,2,1,0:T(8,128)(2,1)S(1)} %get-tuple-element.15.x_ref, bf16[64,192]{1,0:T(8,128)(2,1)S(1)} %get-tuple-element.16.fy_ref), custom_call_target="tpu_custom_call" | custom-call | flops 2000000000 | bytes 4194304 | tf_op jit(solution)/shard_map/own_cells/pallas_call | solution.py:486
  15.8 0.0 copy-start.2
  15.9 0.0 copy-start.3
  15.9 0.0 copy-start.4
  15.9 0.0 copy-start.5
  15.9 0.0 collective-permute-done.depth_ref
  15.9 0.9 modes.1
  16.8 14.0 %all_to_all.20 = bf16[16,128,128]{2,1,0:T(8,128)(2,1)S(1)} all-to-all(bf16[16,128,128]{2,1,0:T(8,128)(2,1)S(1)} %bitcast.15), channel_id=1, replica_groups=mesh['zl'=4,'x'=4,'c'=2,'zh'=4,'y'=4] {'y','x'}, dimensions={0} | all-to-all | bytes 1048576 | tf_op jit(solution)/shard_map/all_to_all | solution.py:503
  30.8 0.0 copy-start
  30.8 0.0 copy-start.1
  30.8 0.1 convert_reduce_fusion
  30.9 26.7 %all_to_all.21 = f32[32,4,128]{2,1,0:T(4,128)S(1)} all-to-all(f32[32,4,128]{2,1,0:T(4,128)S(1)} %bitcast.24), channel_id=1, replica_groups=mesh['zl'=4,'x'=4,'c'=2,'zh'=4,'y'=4] {'zl','zh','c'}, dimensions={0} | all-to-all | bytes 131072 | tf_op jit(solution)/shard_map/all_to_all | solution.py:505
  57.6 0.0 copy-done.2
  57.6 0.0 copy-done.3
  57.6 0.0 copy-done.4
  57.6 0.0 copy-done.5
  57.6 0.9 update.1
  58.6 16.5 %all_to_all.22 = bf16[32,4,128]{2,1,0:T(4,128)(2,1)S(1)} all-to-all(bf16[32,4,128]{2,1,0:T(4,128)(2,1)S(1)} %bitcast.25), channel_id=1, replica_groups=mesh['zl'=4,'x'=4,'c'=2,'zh'=4,'y'=4] {'zl','zh','c'}, dimensions={0} | all-to-all | bytes 65536 | tf_op jit(solution)/shard_map/all_to_all | solution.py:520
  75.1 0.1 broadcast_in_dim.8
  75.2 12.9 %all_to_all.23 = bf16[16,128,128]{2,1,0:T(8,128)(2,1)S(1)} all-to-all(bf16[16,128,128]{2,1,0:T(8,128)(2,1)S(1)} %broadcast_in_dim.8), channel_id=1, replica_groups=mesh['zl'=4,'x'=4,'c'=2,'zh'=4,'y'=4] {'y','x'}, dimensions={0} | all-to-all | bytes 1048576 | tf_op jit(solution)/shard_map/all_to_all | solution.py:522
  88.1 4.1 %collective-permute-start.1 = (bf16[2048,128]{1,0:T(8,128)(2,1)S(1)}, bf16[2048,128]{1,0:T(8,128)(2,1)S(1)}, u32[]{:S(2)}, u32[]{:S(2)}) collective-permute-start(bf16[2048,128]{1,0:T(8,128)(2,1)S(1)} %bitcast.16), channel_id=1, source_target_pairs={{0,16},{16,0},{1,17},{17,1},{2,18},{18,2},{3,19},{19,3},{4,20},{20... | collective-permute-start | bytes 1572872 | tf_op jit(solution)/shard_map/ppermute | solution.py:523
  92.2 0.0 copy-done
  92.2 0.0 copy-done.1
  92.2 2.5 %expand_own.1.part_ref = f32[512,1024]{1,0:T(8,128)S(1)} custom-call(s32[3]{0:T(128)S(1)} %pad_add_fusion.at_ref, bf16[2048,128]{1,0:T(8,128)(2,1)S(1)} %bitcast.17, bf16[512,1024]{1,0:T(8,128)(2,1)S(1)} %get-tuple-element.13.slope_ref, bf16[256,256]{1,0:T(8,128)(2,1)S(1)} %get-tuple-element.18.l_ref, bf16[2,256,1024]{2,1,0:T(8,128)(2,1)S(1)} %copy-done.1, ...), custom_call_target="tpu_custom_call" | custom-call | flops 3000000000 | bytes 4194304 | tf_op jit(solution)/shard_map/expand_own/pallas_call | solution.py:526
  94.7 0.0 collective-permute-done.1.modes_ref
  94.7 3.3 %expand.1 = f32[512,1024]{1,0:T(8,128)} custom-call(s32[3]{0:T(128)S(1)} %pad_add_fusion.at_ref, bf16[2048,128]{1,0:T(8,128)(2,1)S(1)} %collective-permute-done.1.modes_ref, f32[512,1024]{1,0:T(8,128)S(1)} %expand_own.1.part_ref, bf16[2,256,1024]{2,1,0:T(8,128)(2,1)S(1)} %copy-done.1, bf16[2,256,1024]{2,1,0:T(8,128)(2,1)S(1)} %copy-done, ...), custom_call_target="tpu_custom_call" | custom-call | bytes 4194304 | tf_op jit(solution)/shard_map/expand/pallas_call | solution.py:535
  (1 shorter events, 0.0 us)
Async XLA Ops:
  5.3 10.6 %collective-permute-start = (f32[512,256]{1,0:T(8,128)S(1)}, f32[512,256]{1,0:T(8,128)S(1)}, u32[]{:S(2)}, u32[]{:S(2)}) collective-permute-start(f32[512,256]{1,0:T(8,128)S(1)} %get-tuple-element.12), channel_id=1, source_target_pairs={{0,16},{16,0},{1,17},{17,1},{2,18},{18,2},{3,19},{19,3},{4,20},{20... | collective-permute-start | bytes 1572872 | tf_op jit(solution)/shard_map/ppermute | solution.py:485
  15.8 41.7 %copy-start.2 = (bf16[128,2048]{1,0:T(8,128)(2,1)S(1)}, bf16[128,2048]{1,0:T(8,128)(2,1)}, u32[]{:S(2)}) copy-start(bf16[128,2048]{1,0:T(8,128)(2,1)} %constant.52.clone.spread_c_ref) | copy-start | bytes 1572868
  15.9 41.7 %copy-start.3 = (bf16[128,2048]{1,0:T(8,128)(2,1)S(1)}, bf16[128,2048]{1,0:T(8,128)(2,1)}, u32[]{:S(2)}) copy-start(bf16[128,2048]{1,0:T(8,128)(2,1)} %constant.51.clone.spread_o_ref) | copy-start | bytes 1572868
  15.9 41.7 %copy-start.4 = (f32[1,2,8192]{2,1,0:T(2,128)S(1)}, f32[1,2,8192]{2,1,0:T(2,128)}, u32[]{:S(2)}) copy-start(f32[1,2,8192]{2,1,0:T(2,128)} %param.16) | copy-start | bytes 196612
  15.9 41.7 %copy-start.5 = (f32[1,2,512]{2,1,0:T(2,128)S(1)}, f32[1,2,512]{2,1,0:T(2,128)}, u32[]{:S(2)}) copy-start(f32[1,2,512]{2,1,0:T(2,128)} %param.15) | copy-start | bytes 12292
  30.8 61.4 %copy-start = (bf16[2,256,1024]{2,1,0:T(8,128)(2,1)S(1)}, bf16[2,256,1024]{2,1,0:T(8,128)(2,1)}, u32[]{:S(2)}) copy-start(bf16[2,256,1024]{2,1,0:T(8,128)(2,1)} %constant.50.clone.low_ref) | copy-start | bytes 3145732
  30.8 61.4 %copy-start.1 = (bf16[2,256,1024]{2,1,0:T(8,128)(2,1)S(1)}, bf16[2,256,1024]{2,1,0:T(8,128)(2,1)}, u32[]{:S(2)}) copy-start(bf16[2,256,1024]{2,1,0:T(8,128)(2,1)} %constant.49.clone.high_ref) | copy-start | bytes 3145732
  88.1 6.6 %collective-permute-start.1 = (bf16[2048,128]{1,0:T(8,128)(2,1)S(1)}, bf16[2048,128]{1,0:T(8,128)(2,1)S(1)}, u32[]{:S(2)}, u32[]{:S(2)}) collective-permute-start(bf16[2048,128]{1,0:T(8,128)(2,1)S(1)} %bitcast.16), channel_id=1, source_target_pairs={{0,16},{16,0},{1,17},{17,1},{2,18},{18,2},{3,19},{19,3},{4,20},{20... | collective-permute-start | bytes 1572872 | tf_op jit(solution)/shard_map/ppermute | solution.py:523

commit v3 on v2

--- a/solution.py
+++ b/solution.py
@@ -19,13 +19,16 @@
 HALF = KZ * CH
 QUARTER = 128
 ROWS = TILE_X * TILE_Y
-CHUNKS = 8
+CHUNKS = 4
 CHUNK_ROWS = ROWS // CHUNKS
 NORM = 1.0 / math.sqrt(NX * NY * DEPTH)
 F32, BF16 = jnp.float32, jnp.bfloat16
 MIB = 1024 * 1024
 PLANE = ("y", "x")
 LINE = ("zl", "zh", "c")
+FAR = 2
+LINE_ORDER = [[(zl * ZH + (zh ^ FAR)) * CS + c for zl in range(ZL) for zh in range(ZH) for c in range(CS)]]
+PLANE_ORDER = [[(y ^ FAR) * XS + (x ^ FAR) for y in range(YS) for x in range(XS)]]
 
 
 def split_table(table):
@@ -34,49 +37,9 @@
     return high, low
 
 
-def mode_ids(count, length):
-    ordinal = np.arange(count)
-    return np.where(ordinal < count // 2, ordinal, ordinal + length - count)
-
-
-def phase(positions, modes, length):
-    angle = (np.outer(modes, positions) % length) * (2.0 * np.pi / length)
-    return np.cos(angle), np.sin(angle)
-
-
-KX_ORDER = np.array([zl * 8 + x * 2 + c for x in range(XS) for zl in range(ZL) for c in range(CS)])
-KY_ORDER = np.array([zh * 8 + y * 2 + k for y in range(YS) for zh in range(ZH) for k in range(2)])
-
-
-def rotation(cosine, sine):
-    return np.stack([np.stack([cosine, sine]), np.stack([-sine, cosine])])
-
-
 @functools.cache
 def tables():
-    ky = mode_ids(KY, NY)[KY_ORDER]
-    kx = mode_ids(KX, NX)[KX_ORDER]
-    forward_y, inverse_y, forward_x = [], [], []
-    for tile in range(NY // TILE_Y):
-        turn = rotation(*phase(tile * TILE_Y + np.arange(TILE_Y), ky, NY))
-        turn = turn.reshape(2, 2, YS, 8, TILE_Y)
-        rows = turn.transpose(2, 0, 3, 1, 4).reshape(2 * KY, 2 * TILE_Y)
-        high, low = split_table(rows)
-        forward_y.append(np.concatenate([high, high, low], 1))
-        high, low = split_table(rows.reshape(2 * KY, 2, TILE_Y).transpose(1, 2, 0).reshape(2 * TILE_Y, -1))
-        inverse_y.append(np.concatenate([high, high, low], 1))
-    for tile in range(NX // TILE_X):
-        parts = []
-        for source in (tile, tile ^ 1):
-            turn = rotation(*phase(source * TILE_X + np.arange(TILE_X), kx, NX))
-            parts.append(turn.transpose(2, 0, 3, 1).reshape(2 * KX, 2 * TILE_X))
-        forward_x.append(np.concatenate(split_table(np.concatenate(parts, 1)), 1))
     depth_angle = (np.outer(np.arange(DEPTH), np.arange(KZ)) % DEPTH) * (2.0 * np.pi / DEPTH)
-    weight = np.where(np.arange(KZ) == 0, 1.0, 2.0)
-    factor = np.stack([np.cos(depth_angle) * weight, -np.sin(depth_angle) * weight], 1)
-    factor = factor.astype(np.float32).astype(ml_dtypes.bfloat16).astype(np.float32)
-    project = np.repeat(factor.reshape(DEPTH, 2, 2, 8).transpose(2, 0, 1, 3), CH, 3)
-    project = project.reshape(2, DEPTH, HALF).astype(ml_dtypes.bfloat16)
     expand = np.stack([np.cos(depth_angle).T, -np.sin(depth_angle).T], 0) * NORM
     expand = expand.reshape(2, 2, 8, DEPTH).transpose(1, 0, 2, 3).reshape(2, KZ, DEPTH)
     expand = np.stack([np.kron(part, np.eye(CH)) for part in expand])
@@ -85,10 +48,6 @@
     spread_o = np.kron(kz8, np.kron(ones, eye)).astype(ml_dtypes.bfloat16)
     spread_c = np.kron(kz8, np.kron(eye, ones)).astype(ml_dtypes.bfloat16)
     return dict(
-        forward_y=np.stack(forward_y),
-        inverse_y=np.stack(inverse_y),
-        forward_x=np.stack(forward_x),
-        project=project,
         expand_high=expand_high,
         expand_low=expand_low,
         spread_o=spread_o,
@@ -194,24 +153,71 @@
     out_ref[...] = jnp.where(same, full, 0.0).astype(BF16)
 
 
-def fill_project(f_ref, table_ref, half):
+def turn(units):
+    distance = jnp.abs((units + 256 & 511) - 256)
+    far = distance > 128
+    near = jnp.where(far, 256 - distance, distance)
+    square = near.astype(F32) * (2.0 * math.pi / 512)
+    square = square * square
+    value = jnp.full(units.shape, 1.0 / math.factorial(12), F32)
+    for power in (10, 8, 6, 4, 2, 0):
+        value = value * square + (-1.0) ** (power // 2) / math.factorial(power)
+    value = jnp.where(near == 128, 0.0, value)
+    return jnp.where(far, -value, value)
+
+
+def mode_of(ordinal):
+    return jnp.where(ordinal < 16, ordinal, ordinal - 32)
+
+
+def x_table(tile):
+    shape = (2 * KX, 8 * TILE_X)
+    row, column = iota(shape, 0), iota(shape, 1)
+    mode = mode_of((row >> 2 & 3) * 8 + ((row >> 4) ^ FAR) * 2 + (row >> 1 & 1))
+    cell = (tile ^ (column >> 5 & 1)) * TILE_X + (column >> 1 & 15)
+    value = turn(mode * cell + 128 * ((row & 1) - (column & 1)))
+    high = value.astype(BF16)
+    low = (value - high.astype(F32)).astype(BF16)
+    return jnp.where(column < 4 * TILE_X, high.astype(F32), low.astype(F32)).astype(BF16)
+
+
+def y_table(tile, inverse):
+    shape = (64, 192)
+    mode, cell = iota(shape, 0), iota(shape, 1)
+    column = cell
+    if inverse:
+        mode, cell = cell, mode
+    ordinal = ((mode >> 1 & 3) ^ FAR) * 8 + ((mode >> 4 & 3) ^ FAR) * 2 + (mode & 1)
+    place = tile * TILE_Y + (cell & 31)
+    value = turn(mode_of(ordinal) * place + 128 * ((mode >> 3 & 1) - (cell >> 5 & 1)))
+    high = value.astype(BF16)
+    low = (value - high.astype(F32)).astype(BF16)
+    return jnp.where(column < 128, high.astype(F32), low.astype(F32)).astype(BF16)
+
+
+def fill_project(f_ref, half):
+    shape = (DEPTH, HALF)
+    z, column = iota(shape, 0), iota(shape, 1)
+    kz = half * 8 + (column >> 4 & 7)
+    factor = turn((kz * z & 63) * 8 + 128 * (column >> 7))
+    factor = jnp.where(kz == 0, factor, 2.0 * factor)
     shape = (CH, HALF)
     same = iota(shape, 0) == (iota(shape, 1) & (CH - 1))
-    table = table_ref[half].astype(F32)
     for z in range(DEPTH):
-        factor = jnp.broadcast_to(table[z : z + 1], shape)
-        f_ref[z * CH : (z + 1) * CH, :] = jnp.where(same, factor, 0.0).astype(BF16)
+        rows = jnp.broadcast_to(factor[z : z + 1], shape)
+        f_ref[z * CH : (z + 1) * CH, :] = jnp.where(same, rows, 0.0).astype(BF16)
+
+
+def place_of():
+    core = lax.axis_index("c")
+    x_tile = (lax.axis_index("zl") * XS + lax.axis_index("x")) * CS + core
+    return x_tile, lax.axis_index("zh") * YS + lax.axis_index("y"), core
 
 
 def slope_kernel(
-    at_ref,
     cot_hbm,
     pre_hbm,
     local_hbm,
-    table_hbm,
-    fx_hbm,
-    fy_hbm,
-    iy_hbm,
     slope_ref,
     send_ref,
     own_ref,
@@ -223,11 +229,9 @@
     cot_ref,
     pre_ref,
     local_ref,
-    table_ref,
-    fx_ref,
     f_ref,
     sems,
-    small_sems,
+    local_sem,
 ):
     def copies(chunk):
         rows = pl.ds(chunk * CHUNK_ROWS, CHUNK_ROWS)
@@ -236,29 +240,20 @@
             pltpu.make_async_copy(pre_hbm.at[rows], pre_ref.at[rows], sems.at[1, chunk]),
         )
 
-    small = [
-        pltpu.make_async_copy(source, target, small_sems.at[i])
-        for i, (source, target) in enumerate(
-            (
-                (fx_hbm.at[at_ref[0]], fx_ref),
-                (table_hbm, table_ref),
-                (local_hbm, local_ref),
-                (fy_hbm.at[at_ref[1]], fy_ref),
-                (iy_hbm.at[at_ref[1]], iy_ref),
-            )
-        )
-    ]
-    for copy in small:
-        copy.start()
     for chunk in range(CHUNKS):
         for copy in copies(chunk):
             copy.start()
-    for copy in small:
-        copy.wait()
-    fill_project(f_ref, table_ref, 1 - at_ref[2])
-    fill_project(own_ref, table_ref, at_ref[2])
-    fill_forward(forward_ref, fx_ref[...])
-    fill_inverse(inverse_ref, fx_ref[...])
+    local_copy = pltpu.make_async_copy(local_hbm, local_ref, local_sem)
+    local_copy.start()
+    x_tile, y_tile, core = place_of()
+    fill_project(f_ref, 1 - core)
+    fill_project(own_ref, core)
+    small = x_table(x_tile)
+    fill_forward(forward_ref, small)
+    fill_inverse(inverse_ref, small)
+    fy_ref[...] = y_table(y_tile, False)
+    iy_ref[...] = y_table(y_tile, True)
+    local_copy.wait()
     fill_local(l_ref, local_ref)
     for chunk in range(CHUNKS):
         for copy in copies(chunk):
@@ -332,40 +327,34 @@
         sg_ref[:, half] = jnp.broadcast_to(rows[None], (ZL * ZH, 4, QUARTER))
 
 
-def turn_back(modes_ref, table_high, table_low, iy_ref, wide_ref, rhs_ref):
+def turn_back(modes_ref, wide_ref):
     for y in range(YS):
         wide_ref[:, lanes_of(y)] = modes_ref[y * BLOCK : (y + 1) * BLOCK, :]
-    turned = dot(table_high, wide_ref[...]) + dot(table_low, wide_ref[...])
-    for x in range(TILE_X):
+
+
+def cells_of(first, count, x_ref, iy_ref, wide_ref, rhs_ref):
+    rows = slice(first * 16, (first + count) * 16)
+    turned = dot(x_ref[0, rows, :], wide_ref[...]) + dot(x_ref[1, rows, :], wide_ref[...])
+    for x in range(count):
         for y in range(YS):
             high, low = split(turned[x * 16 : (x + 1) * 16, lanes_of(y)])
             for at, part in enumerate((high, low, high)):
                 rows = slice(at * 2 * KY + y * 16, at * 2 * KY + (y + 1) * 16)
-                rhs_ref[rows, lanes_of(x)] = part
-    turned = dot(iy_ref[...], rhs_ref[...])
+                rhs_ref[rows, lanes_of(first + x)] = part
+    turned = dot(iy_ref[...], rhs_ref[:, first * QUARTER : (first + count) * QUARTER])
     cells = [
         jnp.concatenate([turned[:TILE_Y, lanes_of(x)], turned[TILE_Y:, lanes_of(x)]], 1)
-        for x in range(TILE_X)
+        for x in range(count)
     ]
-    return jnp.concatenate(cells, 0)
+    return split(jnp.concatenate(cells, 0))
 
 
 def expand_own_kernel(
-    at_ref,
-    modes_ref,
-    slope_ref,
-    l_ref,
-    high_ref,
-    low_ref,
-    x_ref,
-    iy_ref,
-    out_ref,
-    wide_ref,
-    rhs_ref,
+    modes_ref, slope_ref, l_ref, high_ref, low_ref, x_ref, iy_ref, out_ref, wide_ref, rhs_ref
 ):
-    cells = turn_back(modes_ref, x_ref[0], x_ref[1], iy_ref, wide_ref, rhs_ref)
-    high, low = split(cells)
-    half = at_ref[2]
+    turn_back(modes_ref, wide_ref)
+    high, low = cells_of(0, TILE_X, x_ref, iy_ref, wide_ref, rhs_ref)
+    half = lax.axis_index("c")
     for part in range(4):
         lanes = slice(part * 256, (part + 1) * 256)
         table = high_ref[half, :, lanes]
@@ -378,7 +367,6 @@
 
 
 def expand_kernel(
-    at_ref,
     modes_ref,
     part_ref,
     high_ref,
@@ -391,23 +379,27 @@
     out_ref,
     sems,
 ):
-    cells = turn_back(modes_ref, x_ref[0], x_ref[1], iy_ref, wide_ref, rhs_ref)
-    high, low = split(cells)
-    half = 1 - at_ref[2]
+    turn_back(modes_ref, wide_ref)
+    half = 1 - lax.axis_index("c")
     copies = []
-    for part in range(4):
-        lanes = slice(part * 256, (part + 1) * 256)
-        table = high_ref[half, :, lanes]
-        out_ref[:, lanes] = (
-            dot(high, table)
-            + dot(low, table)
-            + dot(high, low_ref[half, :, lanes])
-            + part_ref[:, lanes]
-        )
-        copies.append(
-            pltpu.make_async_copy(out_ref.at[:, lanes], out_hbm.at[:, lanes], sems.at[part])
-        )
-        copies[-1].start()
+    for step in range(2):
+        count = TILE_X // 2
+        high, low = cells_of(step * count, count, x_ref, iy_ref, wide_ref, rhs_ref)
+        rows = slice(step * ROWS // 2, (step + 1) * ROWS // 2)
+        for part in range(4):
+            lanes = slice(part * 256, (part + 1) * 256)
+            table = high_ref[half, :, lanes]
+            out_ref[rows, lanes] = (
+                dot(high, table)
+                + dot(low, table)
+                + dot(high, low_ref[half, :, lanes])
+                + part_ref[rows, lanes]
+            )
+            copy = pltpu.make_async_copy(
+                out_ref.at[rows, lanes], out_hbm.at[rows, lanes], sems.at[step, part]
+            )
+            copy.start()
+            copies.append(copy)
     for copy in copies:
         copy.wait()
 
@@ -416,7 +408,6 @@
     return [pl.BlockSpec(memory_space=pltpu.VMEM)] * count
 
 
-SMEM = pl.BlockSpec(memory_space=pltpu.SMEM)
 IN_HBM = pl.BlockSpec(memory_space=pltpu.HBM)
 
 
@@ -439,9 +430,6 @@
 
 def on_device(cotangent, preact, spectra, spectral_weight, local_weight):
     table = {name: jnp.asarray(value) for name, value in tables().items()}
-    place = jnp.stack(
-        [lax.axis_index(("zl", "x", "c")), lax.axis_index(("zh", "y")), lax.axis_index("c")]
-    ).astype(jnp.int32)
     swap = [(0, 1), (1, 0)]
     square = (ROWS, HALF)
     turn_scratch = pltpu.VMEM((6 * TILE_Y, TILE_X * QUARTER), BF16)
@@ -460,27 +448,20 @@
             ((2 * KY, 6 * TILE_Y), BF16),
             ((2 * TILE_Y, 6 * KY), BF16),
         ],
-        [SMEM, *[IN_HBM] * 7],
+        [IN_HBM] * 3,
         in_vmem(8),
         [
             pltpu.VMEM((ROWS, ROW), BF16),
             pltpu.VMEM((ROWS, ROW), BF16),
             pltpu.VMEM((CH, CH), BF16),
-            pltpu.VMEM((2, DEPTH, HALF), BF16),
-            pltpu.VMEM((2 * KX, 8 * TILE_X), BF16),
             pltpu.VMEM((ROW, HALF), BF16),
             pltpu.SemaphoreType.DMA((2, CHUNKS)),
-            pltpu.SemaphoreType.DMA((5,)),
+            pltpu.SemaphoreType.DMA,
         ],
     )(
-        place,
         in_hbm(cotangent.reshape(ROWS, ROW)),
         in_hbm(preact.reshape(ROWS, ROW)),
         in_hbm(local_weight),
-        in_hbm(table["project"]),
-        in_hbm(table["forward_x"]),
-        in_hbm(table["forward_y"]),
-        in_hbm(table["inverse_y"]),
     )
     depth = lax.ppermute(send, "c", swap)
     (own,) = call(
@@ -500,9 +481,9 @@
         in_vmem(1),
         [turn_scratch, *cell_scratch],
     )(depth, own, forward_x, forward_y)
-    partial = lax.all_to_all(partial.reshape(16, 128, QUARTER), PLANE, 0, 0, tiled=True)
+    partial = lax.all_to_all(partial.reshape(16, 128, QUARTER), PLANE, 0, 0, tiled=True, axis_index_groups=PLANE_ORDER)
     sums = jnp.sum(partial.astype(F32), 0).reshape(32, 4, QUARTER)
-    sums = lax.all_to_all(sums, LINE, 0, 0, tiled=True)
+    sums = lax.all_to_all(sums, LINE, 0, 0, tiled=True, axis_index_groups=LINE_ORDER)
     grad_weight, back = call(
         update_kernel,
         "update",
@@ -517,9 +498,16 @@
         table["spread_o"],
         table["spread_c"],
     )
-    back = lax.all_to_all(back.reshape(32, 4, QUARTER).astype(BF16), LINE, 0, 0, tiled=True)
+    back = lax.all_to_all(
+        back.reshape(32, 4, QUARTER).astype(BF16),
+        LINE,
+        0,
+        0,
+        tiled=True,
+        axis_index_groups=LINE_ORDER,
+    )
     back = jnp.broadcast_to(back.reshape(1, 128, QUARTER), (16, 128, QUARTER))
-    modes = lax.all_to_all(back, PLANE, 0, 0, tiled=True).reshape(2048, QUARTER)
+    modes = lax.all_to_all(back, PLANE, 0, 0, tiled=True, axis_index_groups=PLANE_ORDER).reshape(2048, QUARTER)
     other = lax.ppermute(modes, "c", swap)
     back_scratch = [pltpu.VMEM((BLOCK, YS * QUARTER), BF16), turn_scratch]
     depth_tables = (table["expand_high"], table["expand_low"])
@@ -527,19 +515,19 @@
         expand_own_kernel,
         "expand_own",
         [((ROWS, ROW), F32)],
-        [SMEM, *in_vmem(7)],
+        in_vmem(7),
         in_vmem(1),
         back_scratch,
         flops=3 * 10**9,
-    )(place, modes, slope, local_map, *depth_tables, inverse_x, inverse_y)
+    )(modes, slope, local_map, *depth_tables, inverse_x, inverse_y)
     (result,) = call(
         expand_kernel,
         "expand",
         [((ROWS, ROW), F32)],
-        [SMEM, *in_vmem(6)],
+        in_vmem(6),
         [IN_HBM],
-        [*back_scratch, pltpu.VMEM((ROWS, ROW), F32), pltpu.SemaphoreType.DMA((4,))],
-    )(place, other, part, *depth_tables, inverse_x, inverse_y)
+        [*back_scratch, pltpu.VMEM((ROWS, ROW), F32), pltpu.SemaphoreType.DMA((2, 4))],
+    )(other, part, *depth_tables, inverse_x, inverse_y)
     return result.reshape(TILE_X, TILE_Y, ROW), grad_weight.reshape(1, 2, 8192)
 
 

time: 98.3 us -> 87.2 us (0.89)
  blocking collectives: 70.1 us -> 62.5 us
  Pallas kernels: 14 us -> 12.2 us
  starting transfers between devices: 12.8 us -> 11.2 us
    all_to_all x3, blocking collectives: 53.6 us -> 47 us  [the longest x1 19.2 us: on_device(): lax.all_to_all(sums, LINE, 0, 0, tiled=True, axis_index_groups=LINE_ORDER)]
    ppermute x1, starting transfers between devices: 4.06 us -> 2.39 us  [on_device(): other = lax.ppermute(modes, 'c', swap)]
    all_to_all x1, blocking collectives: 16.5 us -> 15.5 us  [on_device(): lax.all_to_all(back.reshape(32, 4, QUARTER).astype(BF16), LINE, 0, 0, til...]
where the time goes in v3:
time: 87.2 us; the launch traced here: 86.9 us
  blocking collectives  62.5 us (72%)
  Pallas kernels  12.2 us (14%)
  starting transfers between devices  11.2 us (13%)
    all_to_all x1, blocking collectives, on_device(): lax.all_to_all(sums, LINE, 0, 0, tiled=True, axis_index_groups=LINE_ORDER)  19.2 us
    all_to_all x1, blocking collectives, on_device(): lax.all_to_all(back.reshape(32, 4, QUARTER).astype(BF16), LINE, 0, 0, til...  15.5 us
    all_to_all x1, blocking collectives, on_device(): lax.all_to_all(back, PLANE, 0, 0, tiled=True, axis_index_groups=PLANE_ORDER)  14 us
    all_to_all x1, blocking collectives, on_device(): lax.all_to_all(partial.reshape(16, 128, QUARTER), PLANE, 0, 0, tiled=True...  13.7 us
    ppermute x1, starting transfers between devices, on_device(): depth = lax.ppermute(send, 'c', swap)  8.79 us
    pallas_call x1, Pallas kernels, on_device(): call(slope_kernel, 'slope', [((ROWS, ROW), BF16), (square, F32), ((ROW, H...  3.86 us
    pallas_call x1, Pallas kernels, on_device(): call(expand_kernel, 'expand', [((ROWS, ROW), F32)], in_vmem(6), [IN_HBM],...  2.89 us
    ppermute x1, starting transfers between devices, on_device(): other = lax.ppermute(modes, 'c', swap)  2.39 us
  transfers between devices with their start and end apart: 2, of which 0 were waited for; matrix products, arithmetic and copies ran while one was open for 0% of the time, Pallas kernels for 4%

profile of v3, /device:TPU:1, one launch (start us, length us, event | category | flops | bytes accessed | tf_op | source)
XLA Modules:
  0.0 86.9 jit_solution(8285352357224591455)
XLA Ops:
  0.6 3.9 %slope.1 = (bf16[512,1024]{1,0:T(8,128)(2,1)S(1)}, f32[512,256]{1,0:T(8,128)S(1)}, bf16[1024,256]{1,0:T(8,128)(2,1)S(1)}, bf16[2,2,512,256]{3,2,1,0:T(8,128)(2,1...) custom-call(bf16[512,1024]{1,0:T(8,128)(2,1)} %bitcast.19, ...), custom_call_target="tpu_custom_call" | custom-call | bytes 4194304 | tf_op jit(solution)/shard_map/slope/pallas_call | solution.py:438
  4.5 8.8 %collective-permute-start = (f32[512,256]{1,0:T(8,128)S(1)}, f32[512,256]{1,0:T(8,128)S(1)}, u32[]{:S(2)}, u32[]{:S(2)}) collective-permute-start(f32[512,256]{1,0:T(8,128)S(1)} %get-tuple-element.12), channel_id=1, source_target_pairs={{0,16},{16,0},{1,17},{17,1},{2,18},{18,2},{3,19},{19,3},{4,20},{20... | collective-permute-start | bytes 1572872 | tf_op jit(solution)/shard_map/ppermute | solution.py:466
  13.3 1.7 %own_cells.1.part_ref = f32[512,512]{1,0:T(8,128)S(1)} custom-call(bf16[512,1024]{1,0:T(8,128)(2,1)S(1)} %get-tuple-element.13.slope_ref, bf16[1024,256]{1,0:T(8,128)(2,1)S(1)} %get-tuple-element.14.f_ref, bf16[2,2,512,256]{3,2,1,0:T(8,128)(2,1)S(1)} %get-tuple-element.15.x_ref, bf16[64,192]{1,0:T(8,128)(2,1)S(1)} %get-tuple-element.16.fy_ref), custom_call_target="tpu_custom_call" | custom-call | flops 2000000000 | bytes 4194304 | tf_op jit(solution)/shard_map/own_cells/pallas_call | solution.py:467
  15.0 0.0 copy-start.2
  15.0 0.0 copy-start.3
  15.0 0.0 copy-start.4
  15.1 0.0 copy-start.5
  15.1 0.0 collective-permute-done.depth_ref
  15.1 0.9 %modes.1 = bf16[2048,128]{1,0:T(8,128)(2,1)S(1)} custom-call(f32[512,256]{1,0:T(8,128)S(1)} %collective-permute-done.depth_ref, f32[512,512]{1,0:T(8,128)S(1)} %own_cells.1.part_ref, bf16[2,2,512,256]{3,2,1,0:T(8,128)(2,1)S(1)} %get-tuple-element.15.x_ref, bf16[64,192]{1,0:T(8,128)(2,1)S(1)} %get-tuple-element.16.fy_ref), custom_call_target="tpu_custom_call" | custom-call | bytes 4194304 | tf_op jit(solution)/shard_map/modes/pallas_call | solution.py:476
  16.0 13.7 %all_to_all.20 = bf16[16,128,128]{2,1,0:T(8,128)(2,1)S(1)} all-to-all(bf16[16,128,128]{2,1,0:T(8,128)(2,1)S(1)} %bitcast.12), channel_id=1, replica_groups={{66,98,2,34,67,99,3,35,64,96,0,32,65,97,1,33},{70,102,6,38,71,103,7,39,..., dimensions={0} | all-to-all | bytes 1048576 | tf_op jit(solution)/shard_map/all_to_all | solution.py:484
  29.8 0.0 copy-start
  29.8 0.0 copy-start.1
  29.8 0.1 convert_reduce_fusion
  29.8 19.2 %all_to_all.21 = f32[32,4,128]{2,1,0:T(4,128)S(1)} all-to-all(f32[32,4,128]{2,1,0:T(4,128)S(1)} %bitcast.21), channel_id=1, replica_groups={{8,24,12,28,0,16,4,20,136,152,140,156,128,144,132,148,264,280,268,284,2..., dimensions={0} | all-to-all | bytes 131072 | tf_op jit(solution)/shard_map/all_to_all | solution.py:486
  49.1 0.0 copy-done.2
  49.1 0.0 copy-done.3
  49.1 0.0 copy-done.4
  49.1 0.0 copy-done.5
  49.1 0.9 %update.1 = (f32[2,8192]{1,0:T(2,128)}, f32[16,2,4,128]{3,2,1,0:T(4,128)S(1)}) custom-call(f32[16,2,4,128]{3,2,1,0:T(4,128)S(1)} %bitcast.15, f32[2,512]{1,0:T(2,128)S(1)} %bitcast.17, f32[2,8192]{1,0:T(2,128)S(1)} %bitcast.16, bf16[128,2048]{1,0:T(8,128)(2,1)S(1)} %copy-done.3, bf16[128,2048]{1,0:T(8,128)(2,1)S(1)} %copy-done.2), custom_call_target="tpu_custom_call" | custom-call | bytes 4194304 | tf_op jit(solution)/shard_map/update/pallas_call | solution.py:487
  50.0 15.5 %all_to_all.22 = bf16[32,4,128]{2,1,0:T(4,128)(2,1)S(1)} all-to-all(bf16[32,4,128]{2,1,0:T(4,128)(2,1)S(1)} %bitcast.22), channel_id=1, replica_groups={{8,24,12,28,0,16,4,20,136,152,140,156,128,144,132,148,264,280,268,284,2..., dimensions={0} | all-to-all | bytes 65536 | tf_op jit(solution)/shard_map/all_to_all | solution.py:501
  65.5 0.1 broadcast_in_dim.8
  65.6 14.0 %all_to_all.23 = bf16[16,128,128]{2,1,0:T(8,128)(2,1)S(1)} all-to-all(bf16[16,128,128]{2,1,0:T(8,128)(2,1)S(1)} %broadcast_in_dim.8), channel_id=1, replica_groups={{66,98,2,34,67,99,3,35,64,96,0,32,65,97,1,33},{70,102,6,38,71,103,7,39,..., dimensions={0} | all-to-all | bytes 1048576 | tf_op jit(solution)/shard_map/all_to_all | solution.py:510
  79.6 2.4 %collective-permute-start.1 = (bf16[2048,128]{1,0:T(8,128)(2,1)S(1)}, bf16[2048,128]{1,0:T(8,128)(2,1)S(1)}, u32[]{:S(2)}, u32[]{:S(2)}) collective-permute-start(bf16[2048,128]{1,0:T(8,128)(2,1)S(1)} %bitcast.13), channel_id=1, source_target_pairs={{0,16},{16,0},{1,17},{17,1},{2,18},{18,2},{3,19},{19,3},{4,20},{20... | collective-permute-start | bytes 1572872 | tf_op jit(solution)/shard_map/ppermute | solution.py:511
  82.0 0.0 copy-done
  82.1 0.0 copy-done.1
  82.1 1.9 %expand_own.1.part_ref = f32[512,1024]{1,0:T(8,128)S(1)} custom-call(bf16[2048,128]{1,0:T(8,128)(2,1)S(1)} %bitcast.14, bf16[512,1024]{1,0:T(8,128)(2,1)S(1)} %get-tuple-element.13.slope_ref, bf16[256,256]{1,0:T(8,128)(2,1)S(1)} %get-tuple-element.18.l_ref, bf16[2,256,1024]{2,1,0:T(8,128)(2,1)S(1)} %copy-done.1, bf16[2,256,1024]{2,1,0:T(8,128)(2,1)S(1)} %copy-done, ...), custom_call_target="tpu_custom_call" | custom-call | flops 3000000000 | bytes 4194304 | tf_op jit(solution)/shard_map/expand_own/pallas_call | solution.py:514
  84.0 0.0 collective-permute-done.1.modes_ref
  84.0 2.9 %expand.1 = f32[512,1024]{1,0:T(8,128)} custom-call(bf16[2048,128]{1,0:T(8,128)(2,1)S(1)} %collective-permute-done.1.modes_ref, f32[512,1024]{1,0:T(8,128)S(1)} %expand_own.1.part_ref, bf16[2,256,1024]{2,1,0:T(8,128)(2,1)S(1)} %copy-done.1, bf16[2,256,1024]{2,1,0:T(8,128)(2,1)S(1)} %copy-done, bf16[2,256,512]{2,1,0:T(8,128)(2,1)S(1)} %get-tuple-element.19.x_ref, ...), custom_call_target="tpu_custom_call" | custom-call | bytes 4194304 | tf_op jit(solution)/shard_map/expand/pallas_call | solution.py:523
  (1 shorter events, 0.0 us)
Async XLA Ops:
  4.5 10.6 %collective-permute-start = (f32[512,256]{1,0:T(8,128)S(1)}, f32[512,256]{1,0:T(8,128)S(1)}, u32[]{:S(2)}, u32[]{:S(2)}) collective-permute-start(f32[512,256]{1,0:T(8,128)S(1)} %get-tuple-element.12), channel_id=1, source_target_pairs={{0,16},{16,0},{1,17},{17,1},{2,18},{18,2},{3,19},{19,3},{4,20},{20... | collective-permute-start | bytes 1572872 | tf_op jit(solution)/shard_map/ppermute | solution.py:466
  15.0 34.0 %copy-start.2 = (bf16[128,2048]{1,0:T(8,128)(2,1)S(1)}, bf16[128,2048]{1,0:T(8,128)(2,1)}, u32[]{:S(2)}) copy-start(bf16[128,2048]{1,0:T(8,128)(2,1)} %constant.13.clone.spread_c_ref) | copy-start | bytes 1572868
  15.0 34.0 %copy-start.3 = (bf16[128,2048]{1,0:T(8,128)(2,1)S(1)}, bf16[128,2048]{1,0:T(8,128)(2,1)}, u32[]{:S(2)}) copy-start(bf16[128,2048]{1,0:T(8,128)(2,1)} %constant.12.clone.spread_o_ref) | copy-start | bytes 1572868
  15.0 34.0 %copy-start.4 = (f32[1,2,8192]{2,1,0:T(2,128)S(1)}, f32[1,2,8192]{2,1,0:T(2,128)}, u32[]{:S(2)}) copy-start(f32[1,2,8192]{2,1,0:T(2,128)} %param.12) | copy-start | bytes 196612
  15.1 34.0 %copy-start.5 = (f32[1,2,512]{2,1,0:T(2,128)S(1)}, f32[1,2,512]{2,1,0:T(2,128)}, u32[]{:S(2)}) copy-start(f32[1,2,512]{2,1,0:T(2,128)} %param.11) | copy-start | bytes 12292
  29.8 52.3 %copy-start = (bf16[2,256,1024]{2,1,0:T(8,128)(2,1)S(1)}, bf16[2,256,1024]{2,1,0:T(8,128)(2,1)}, u32[]{:S(2)}) copy-start(bf16[2,256,1024]{2,1,0:T(8,128)(2,1)} %constant.11.clone.low_ref) | copy-start | bytes 3145732
  29.8 52.3 %copy-start.1 = (bf16[2,256,1024]{2,1,0:T(8,128)(2,1)S(1)}, bf16[2,256,1024]{2,1,0:T(8,128)(2,1)}, u32[]{:S(2)}) copy-start(bf16[2,256,1024]{2,1,0:T(8,128)(2,1)} %constant.10.clone.high_ref) | copy-start | bytes 3145732
  79.6 4.3 %collective-permute-start.1 = (bf16[2048,128]{1,0:T(8,128)(2,1)S(1)}, bf16[2048,128]{1,0:T(8,128)(2,1)S(1)}, u32[]{:S(2)}, u32[]{:S(2)}) collective-permute-start(bf16[2048,128]{1,0:T(8,128)(2,1)S(1)} %bitcast.13), channel_id=1, source_target_pairs={{0,16},{16,0},{1,17},{17,1},{2,18},{18,2},{3,19},{19,3},{4,20},{20... | collective-permute-start | bytes 1572872 | tf_op jit(solution)/shard_map/ppermute | solution.py:511

commit v4 on v3

--- a/solution.py
+++ b/solution.py
@@ -19,16 +19,16 @@
 HALF = KZ * CH
 QUARTER = 128
 ROWS = TILE_X * TILE_Y
-CHUNKS = 4
+CHUNKS = 2
 CHUNK_ROWS = ROWS // CHUNKS
 NORM = 1.0 / math.sqrt(NX * NY * DEPTH)
 F32, BF16 = jnp.float32, jnp.bfloat16
 MIB = 1024 * 1024
 PLANE = ("y", "x")
 LINE = ("zl", "zh", "c")
-FAR = 2
+FAR, FAR_PLANE = 2, 2
 LINE_ORDER = [[(zl * ZH + (zh ^ FAR)) * CS + c for zl in range(ZL) for zh in range(ZH) for c in range(CS)]]
-PLANE_ORDER = [[(y ^ FAR) * XS + (x ^ FAR) for y in range(YS) for x in range(XS)]]
+PLANE_ORDER = [[(y ^ FAR_PLANE) * XS + (x ^ FAR_PLANE) for y in range(YS) for x in range(XS)]]
 
 
 def split_table(table):
@@ -44,14 +44,9 @@
     expand = expand.reshape(2, 2, 8, DEPTH).transpose(1, 0, 2, 3).reshape(2, KZ, DEPTH)
     expand = np.stack([np.kron(part, np.eye(CH)) for part in expand])
     expand_high, expand_low = split_table(expand)
-    eye, kz8, ones = np.eye(CH), np.eye(8), np.ones((1, CH))
-    spread_o = np.kron(kz8, np.kron(ones, eye)).astype(ml_dtypes.bfloat16)
-    spread_c = np.kron(kz8, np.kron(eye, ones)).astype(ml_dtypes.bfloat16)
     return dict(
         expand_high=expand_high,
         expand_low=expand_low,
-        spread_o=spread_o,
-        spread_c=spread_c,
     )
 
 
@@ -173,7 +168,7 @@
 def x_table(tile):
     shape = (2 * KX, 8 * TILE_X)
     row, column = iota(shape, 0), iota(shape, 1)
-    mode = mode_of((row >> 2 & 3) * 8 + ((row >> 4) ^ FAR) * 2 + (row >> 1 & 1))
+    mode = mode_of((row >> 2 & 3) * 8 + ((row >> 4) ^ FAR_PLANE) * 2 + (row >> 1 & 1))
     cell = (tile ^ (column >> 5 & 1)) * TILE_X + (column >> 1 & 15)
     value = turn(mode * cell + 128 * ((row & 1) - (column & 1)))
     high = value.astype(BF16)
@@ -187,7 +182,7 @@
     column = cell
     if inverse:
         mode, cell = cell, mode
-    ordinal = ((mode >> 1 & 3) ^ FAR) * 8 + ((mode >> 4 & 3) ^ FAR) * 2 + (mode & 1)
+    ordinal = ((mode >> 1 & 3) ^ FAR) * 8 + ((mode >> 4 & 3) ^ FAR_PLANE) * 2 + (mode & 1)
     place = tile * TILE_Y + (cell & 31)
     value = turn(mode_of(ordinal) * place + 128 * ((mode >> 3 & 1) - (cell >> 5 & 1)))
     high = value.astype(BF16)
@@ -214,25 +209,7 @@
     return x_tile, lax.axis_index("zh") * YS + lax.axis_index("y"), core
 
 
-def slope_kernel(
-    cot_hbm,
-    pre_hbm,
-    local_hbm,
-    slope_ref,
-    send_ref,
-    own_ref,
-    forward_ref,
-    inverse_ref,
-    l_ref,
-    fy_ref,
-    iy_ref,
-    cot_ref,
-    pre_ref,
-    local_ref,
-    f_ref,
-    sems,
-    local_sem,
-):
+def slope_kernel(cot_hbm, pre_hbm, slope_ref, send_ref, cot_ref, pre_ref, f_ref, sems):
     def copies(chunk):
         rows = pl.ds(chunk * CHUNK_ROWS, CHUNK_ROWS)
         return (
@@ -243,18 +220,7 @@
     for chunk in range(CHUNKS):
         for copy in copies(chunk):
             copy.start()
-    local_copy = pltpu.make_async_copy(local_hbm, local_ref, local_sem)
-    local_copy.start()
-    x_tile, y_tile, core = place_of()
-    fill_project(f_ref, 1 - core)
-    fill_project(own_ref, core)
-    small = x_table(x_tile)
-    fill_forward(forward_ref, small)
-    fill_inverse(inverse_ref, small)
-    fy_ref[...] = y_table(y_tile, False)
-    iy_ref[...] = y_table(y_tile, True)
-    local_copy.wait()
-    fill_local(l_ref, local_ref)
+    fill_project(f_ref, 1 - lax.axis_index("c"))
     for chunk in range(CHUNKS):
         for copy in copies(chunk):
             copy.wait()
@@ -262,9 +228,7 @@
         pre_value = pre_ref[rows, :].astype(F32)
         slope = (cot_ref[rows, :].astype(F32) * gelu_slope(pre_value)).astype(BF16)
         slope_ref[rows, :] = slope
-        if (chunk + 1) * 2 % CHUNKS == 0:
-            rows = slice((chunk + 1) * CHUNK_ROWS - ROWS // 2, (chunk + 1) * CHUNK_ROWS)
-            send_ref[rows, :] = dot(slope_ref[rows, :], f_ref[...])
+        send_ref[rows, :] = dot(slope_ref[rows, :], f_ref[...])
 
 
 def turn_y(depth, fy_ref, rhs_ref, high_ref, low_ref):
@@ -284,9 +248,38 @@
     return dot(table_high, high) + dot(table_high, low) + dot(table_low, high)
 
 
-def own_kernel(slope_ref, f_ref, x_ref, fy_ref, part_ref, rhs_ref, high_ref, low_ref):
-    turn_y(dot(slope_ref[...], f_ref[...]), fy_ref, rhs_ref, high_ref, low_ref)
-    part_ref[...] = turn_x(x_ref[0, 0], x_ref[0, 1], high_ref[...], low_ref[...])
+def own_kernel(
+    slope_ref,
+    local_ref,
+    part_ref,
+    forward_ref,
+    inverse_ref,
+    l_ref,
+    fy_ref,
+    iy_ref,
+    f_ref,
+    depth_ref,
+    rhs_ref,
+    high_ref,
+    low_ref,
+):
+    x_tile, y_tile, core = place_of()
+    fill_project(f_ref, core)
+    for chunk in range(4):
+        rows = slice(chunk * ROWS // 4, (chunk + 1) * ROWS // 4)
+        depth_ref[rows, :] = dot(slope_ref[rows, :], f_ref[...])
+    fy_ref[...] = y_table(y_tile, False)
+    iy_ref[...] = y_table(y_tile, True)
+    small = x_table(x_tile)
+    fill_forward(forward_ref, small)
+    fill_inverse(inverse_ref, small)
+    fill_local(l_ref, local_ref)
+    turn_y(depth_ref[...], fy_ref, rhs_ref, high_ref, low_ref)
+    for part in range(2):
+        lanes = slice(part * 256, (part + 1) * 256)
+        part_ref[:, lanes] = turn_x(
+            forward_ref[0, 0], forward_ref[0, 1], high_ref[:, lanes], low_ref[:, lanes]
+        )
 
 
 def modes_kernel(depth_ref, part_ref, x_ref, fy_ref, out_ref, rhs_ref, high_ref, low_ref):
@@ -296,31 +289,50 @@
         out_ref[y * BLOCK : (y + 1) * BLOCK, :] = turned[:, lanes_of(y)].astype(BF16)
 
 
-def update_kernel(
-    sum_ref, spectra_ref, weight_ref, spread_o_ref, spread_c_ref, gw_ref, sg_ref
-):
+def update_kernel(sum_ref, spectra_ref, weight_ref, gw_ref, sg_ref):
     halves = [jnp.sum(sum_ref[:, half], 0) * NORM for half in range(2)]
     grad = jnp.concatenate([halves[0][:2], halves[1][:2], halves[0][2:], halves[1][2:]], 0)
     saved = jnp.concatenate([spectra_ref[:, b * 128 : (b + 1) * 128] for b in range(4)], 0)
-    weight = jnp.concatenate([weight_ref[:, b * 2048 : (b + 1) * 2048] for b in range(4)], 0)
-    grad_wide = sum_parts(dot(three_parts(grad), spread_o_ref[...]))
-    saved_wide = sum_parts(dot(three_parts(saved), spread_c_ref[...]))
+    shape = (64, QUARTER)
+    own_kz = iota(shape, 0) >> 3 == iota(shape, 1) >> 4
+    shape = (QUARTER, CH * CH)
+    row, column = iota(shape, 0) & (CH - 1), iota(shape, 1)
+    spread_c = one_hot(row == column >> 4)
+    spread_o = one_hot(row == (column & (CH - 1)))
+
+    def spread(value, table):
+        rows = jnp.where(own_kz, jnp.concatenate([value] * 8, 0), 0.0)
+        return sum_parts(dot(three_parts(rows), table))
+
+    grad_wide, saved_wide = spread(grad, spread_o), spread(saved, spread_c)
+    weight = jnp.concatenate(
+        [
+            weight_ref[:, b * 2048 + kz * 256 : b * 2048 + (kz + 1) * 256]
+            for kz in range(8)
+            for b in range(4)
+        ],
+        0,
+    )
+    real_rows = (iota((64, CH * CH), 0) & 4) == 0
 
     def combine(value):
-        real, imaginary = value[:4], value[4:]
-        grad_real, grad_imaginary = grad_wide[:4], grad_wide[4:]
-        return jnp.concatenate(
-            [
-                real * grad_real + imaginary * grad_imaginary,
-                real * grad_imaginary - imaginary * grad_real,
-            ],
-            0,
+        product = value * grad_wide
+        crossed = swap_parts(value) * grad_wide
+        return jnp.where(
+            real_rows, product + swap_parts(product), crossed - swap_parts(crossed)
         )
 
+    def swap_parts(value):
+        return jnp.where(real_rows, pltpu.roll(value, 60, 0), pltpu.roll(value, 4, 0))
+
     outer = combine(saved_wide)
-    for b in range(4):
-        gw_ref[:, b * 2048 : (b + 1) * 2048] = outer[2 * b : 2 * b + 2]
-    back = sum_parts(dot_last(three_parts(combine(weight)), spread_c_ref[...]))
+    for kz in range(8):
+        for b in range(4):
+            lanes = slice(b * 2048 + kz * 256, b * 2048 + (kz + 1) * 256)
+            gw_ref[:, lanes] = outer[kz * 8 + b * 2 : kz * 8 + b * 2 + 2]
+    back = sum_parts(dot_last(three_parts(combine(weight)), spread_c))
+    back = jnp.where(own_kz, back, 0.0)
+    back = functools.reduce(jnp.add, [back[kz * 8 : (kz + 1) * 8] for kz in range(8)])
     back = back.astype(BF16).astype(F32)
     for half in range(2):
         rows = jnp.concatenate([back[2 * half : 2 * half + 2], back[2 * half + 4 : 2 * half + 6]], 0)
@@ -373,33 +385,33 @@
     low_ref,
     x_ref,
     iy_ref,
+    gw_ref,
     out_hbm,
+    gw_hbm,
     wide_ref,
     rhs_ref,
     out_ref,
     sems,
+    gw_sem,
 ):
+    gw_copy = pltpu.make_async_copy(gw_ref, gw_hbm, gw_sem)
+    gw_copy.start()
     turn_back(modes_ref, wide_ref)
     half = 1 - lax.axis_index("c")
-    copies = []
-    for step in range(2):
-        count = TILE_X // 2
-        high, low = cells_of(step * count, count, x_ref, iy_ref, wide_ref, rhs_ref)
-        rows = slice(step * ROWS // 2, (step + 1) * ROWS // 2)
-        for part in range(4):
-            lanes = slice(part * 256, (part + 1) * 256)
-            table = high_ref[half, :, lanes]
-            out_ref[rows, lanes] = (
-                dot(high, table)
-                + dot(low, table)
-                + dot(high, low_ref[half, :, lanes])
-                + part_ref[rows, lanes]
-            )
-            copy = pltpu.make_async_copy(
-                out_ref.at[rows, lanes], out_hbm.at[rows, lanes], sems.at[step, part]
-            )
-            copy.start()
-            copies.append(copy)
+    copies = [gw_copy]
+    high, low = cells_of(0, TILE_X, x_ref, iy_ref, wide_ref, rhs_ref)
+    for part in range(4):
+        lanes = slice(part * 256, (part + 1) * 256)
+        table = high_ref[half, :, lanes]
+        out_ref[:, lanes] = (
+            dot(high, table)
+            + dot(low, table)
+            + dot(high, low_ref[half, :, lanes])
+            + part_ref[:, lanes]
+        )
+        copy = pltpu.make_async_copy(out_ref.at[:, lanes], out_hbm.at[:, lanes], sems.at[part])
+        copy.start()
+        copies.append(copy)
     for copy in copies:
         copy.wait()
 
@@ -435,44 +447,36 @@
     turn_scratch = pltpu.VMEM((6 * TILE_Y, TILE_X * QUARTER), BF16)
     cell_scratch = [pltpu.VMEM((CELLS, YS * QUARTER), BF16)] * 2
 
-    slope, send, own_project, forward_x, inverse_x, local_map, forward_y, inverse_y = call(
+    slope, send = call(
         slope_kernel,
         "slope",
+        [((ROWS, ROW), BF16), (square, F32)],
+        [IN_HBM] * 2,
+        in_vmem(2),
         [
-            ((ROWS, ROW), BF16),
-            (square, F32),
-            ((ROW, HALF), BF16),
+            pltpu.VMEM((ROWS, ROW), BF16),
+            pltpu.VMEM((ROWS, ROW), BF16),
+            pltpu.VMEM((ROW, HALF), BF16),
+            pltpu.SemaphoreType.DMA((2, CHUNKS)),
+        ],
+    )(in_hbm(cotangent.reshape(ROWS, ROW)), in_hbm(preact.reshape(ROWS, ROW)))
+    depth = lax.ppermute(send, "c", swap)
+    own, forward_x, inverse_x, local_map, forward_y, inverse_y = call(
+        own_kernel,
+        "own_cells",
+        [
+            ((BLOCK, YS * QUARTER), F32),
             ((2, 2, BLOCK, CELLS), BF16),
             ((2, CELLS, BLOCK), BF16),
             ((16 * CH, 16 * CH), BF16),
             ((2 * KY, 6 * TILE_Y), BF16),
             ((2 * TILE_Y, 6 * KY), BF16),
         ],
-        [IN_HBM] * 3,
-        in_vmem(8),
-        [
-            pltpu.VMEM((ROWS, ROW), BF16),
-            pltpu.VMEM((ROWS, ROW), BF16),
-            pltpu.VMEM((CH, CH), BF16),
-            pltpu.VMEM((ROW, HALF), BF16),
-            pltpu.SemaphoreType.DMA((2, CHUNKS)),
-            pltpu.SemaphoreType.DMA,
-        ],
-    )(
-        in_hbm(cotangent.reshape(ROWS, ROW)),
-        in_hbm(preact.reshape(ROWS, ROW)),
-        in_hbm(local_weight),
-    )
-    depth = lax.ppermute(send, "c", swap)
-    (own,) = call(
-        own_kernel,
-        "own_cells",
-        [((BLOCK, YS * QUARTER), F32)],
-        in_vmem(4),
-        in_vmem(1),
-        [turn_scratch, *cell_scratch],
+        in_vmem(2),
+        in_vmem(6),
+        [pltpu.VMEM((ROW, HALF), BF16), pltpu.VMEM(square, F32), turn_scratch, *cell_scratch],
         flops=2 * 10**9,
-    )(slope, own_project, forward_x, forward_y)
+    )(slope, local_weight)
     (partial,) = call(
         modes_kernel,
         "modes",
@@ -488,15 +492,13 @@
         update_kernel,
         "update",
         [((2, 8192), F32), ((ZL * ZH, CS, 4, QUARTER), F32)],
-        in_vmem(5),
+        in_vmem(3),
         in_vmem(2),
         [],
     )(
         sums.reshape(ZL * ZH, CS, 4, QUARTER),
         spectra.reshape(2, 2 * HALF),
         spectral_weight.reshape(2, 8192),
-        table["spread_o"],
-        table["spread_c"],
     )
     back = lax.all_to_all(
         back.reshape(32, 4, QUARTER).astype(BF16),
@@ -520,14 +522,19 @@
         back_scratch,
         flops=3 * 10**9,
     )(modes, slope, local_map, *depth_tables, inverse_x, inverse_y)
-    (result,) = call(
+    result, grad_weight = call(
         expand_kernel,
         "expand",
-        [((ROWS, ROW), F32)],
-        in_vmem(6),
-        [IN_HBM],
-        [*back_scratch, pltpu.VMEM((ROWS, ROW), F32), pltpu.SemaphoreType.DMA((2, 4))],
-    )(other, part, *depth_tables, inverse_x, inverse_y)
+        [((ROWS, ROW), F32), ((2, 8192), F32)],
+        in_vmem(7),
+        [IN_HBM, IN_HBM],
+        [
+            *back_scratch,
+            pltpu.VMEM((ROWS, ROW), F32),
+            pltpu.SemaphoreType.DMA((4,)),
+            pltpu.SemaphoreType.DMA,
+        ],
+    )(other, part, *depth_tables, inverse_x, inverse_y, grad_weight)
     return result.reshape(TILE_X, TILE_Y, ROW), grad_weight.reshape(1, 2, 8192)
 
 

time: 87.2 us -> 85.3 us (0.978)
  Pallas kernels: 12.2 us -> 10.4 us
    pallas_call x3, Pallas kernels: 8.47 us -> 7.11 us  [the longest x1 2.73 us: on_device(): call(expand_kernel, 'expand', [((ROWS, ROW), F32), ((2, 8192), F32)], in_...]
where the time goes in v4:
time: 85.3 us; the launch traced here: 85 us
  blocking collectives  62.4 us (73%)
  starting transfers between devices  11.2 us (13%)
  Pallas kernels  10.4 us (12%)
    all_to_all x1, blocking collectives, on_device(): lax.all_to_all(sums, LINE, 0, 0, tiled=True, axis_index_groups=LINE_ORDER)  19.1 us
    all_to_all x1, blocking collectives, on_device(): lax.all_to_all(back.reshape(32, 4, QUARTER).astype(BF16), LINE, 0, 0, til...  15.5 us
    all_to_all x1, blocking collectives, on_device(): lax.all_to_all(back, PLANE, 0, 0, tiled=True, axis_index_groups=PLANE_ORDER)  14 us
    all_to_all x1, blocking collectives, on_device(): lax.all_to_all(partial.reshape(16, 128, QUARTER), PLANE, 0, 0, tiled=True...  13.9 us
    ppermute x1, starting transfers between devices, on_device(): depth = lax.ppermute(send, 'c', swap)  8.79 us
    pallas_call x1, Pallas kernels, on_device(): call(expand_kernel, 'expand', [((ROWS, ROW), F32), ((2, 8192), F32)], in_...  2.73 us
    pallas_call x1, Pallas kernels, on_device(): call(slope_kernel, 'slope', [((ROWS, ROW), BF16), (square, F32)], [IN_HBM...  2.54 us
    ppermute x1, starting transfers between devices, on_device(): other = lax.ppermute(modes, 'c', swap)  2.39 us
  transfers between devices with their start and end apart: 2, of which 0 were waited for; matrix products, arithmetic and copies ran while one was open for 0% of the time, Pallas kernels for 4%

profile of v4, /device:TPU:1, one launch (start us, length us, event | category | flops | bytes accessed | tf_op | source)
XLA Modules:
  0.0 85.0 jit_solution(13510307325962525064)
XLA Ops:
  0.6 0.0 copy-start.4
  0.6 2.5 %slope.1 = (bf16[512,1024]{1,0:T(8,128)(2,1)S(1)}, f32[512,256]{1,0:T(8,128)S(1)}) custom-call(bf16[512,1024]{1,0:T(8,128)(2,1)} %bitcast.18, bf16[512,1024]{1,0:T(8,128)(2,1)} %bitcast.19), custom_call_target="tpu_custom_call" | custom-call | bytes 4194304 | tf_op jit(solution)/shard_map/slope/pallas_call | solution.py:450
  3.2 8.8 %collective-permute-start = (f32[512,256]{1,0:T(8,128)S(1)}, f32[512,256]{1,0:T(8,128)S(1)}, u32[]{:S(2)}, u32[]{:S(2)}) collective-permute-start(f32[512,256]{1,0:T(8,128)S(1)} %get-tuple-element.14), channel_id=1, source_target_pairs={{0,16},{16,0},{1,17},{17,1},{2,18},{18,2},{3,19},{19,3},{4,20},{20... | collective-permute-start | bytes 1572872 | tf_op jit(solution)/shard_map/ppermute | solution.py:463
  12.0 0.0 copy-done.4
  12.0 1.8 %own_cells.1 = (f32[512,512]{1,0:T(8,128)S(1)}, bf16[2,2,512,256]{3,2,1,0:T(8,128)(2,1)S(1)}, bf16[2,256,512]{2,1,0:T(8,128)(2,1)S(1)}, bf16[256,256]{1,0:T(8,12...) custom-call(bf16[512,1024]{1,0:T(8,128)(2,1)S(1)} %get-tuple-element.15.slope_ref, ...), custom_call_target="tpu_custom_call" | custom-call | flops 2000000000 | bytes 4194304 | tf_op jit(solution)/shard_map/own_cells/pallas_call | solution.py:464
  13.8 0.0 collective-permute-done.depth_ref
  13.8 0.0 copy-start.2
  13.9 0.0 copy-start.3
  13.9 0.9 %modes.1 = bf16[2048,128]{1,0:T(8,128)(2,1)S(1)} custom-call(f32[512,256]{1,0:T(8,128)S(1)} %collective-permute-done.depth_ref, f32[512,512]{1,0:T(8,128)S(1)} %get-tuple-element.16.part_ref, bf16[2,2,512,256]{3,2,1,0:T(8,128)(2,1)S(1)} %get-tuple-element.17.x_ref, bf16[64,192]{1,0:T(8,128)(2,1)S(1)} %get-tuple-element.18.fy_ref), custom_call_target="tpu_custom_call" | custom-call | bytes 4194304 | tf_op jit(solution)/shard_map/modes/pallas_call | solution.py:480
  14.8 0.0 copy-start
  14.8 0.0 copy-start.1
  14.8 13.9 %all_to_all.20 = bf16[16,128,128]{2,1,0:T(8,128)(2,1)S(1)} all-to-all(bf16[16,128,128]{2,1,0:T(8,128)(2,1)S(1)} %bitcast.12), channel_id=1, replica_groups={{66,98,2,34,67,99,3,35,64,96,0,32,65,97,1,33},{70,102,6,38,71,103,7,39,..., dimensions={0} | all-to-all | bytes 1048576 | tf_op jit(solution)/shard_map/all_to_all | solution.py:488
  28.7 0.1 convert_reduce_fusion
  28.8 19.1 %all_to_all.21 = f32[32,4,128]{2,1,0:T(4,128)S(1)} all-to-all(f32[32,4,128]{2,1,0:T(4,128)S(1)} %bitcast.20), channel_id=1, replica_groups={{8,24,12,28,0,16,4,20,136,152,140,156,128,144,132,148,264,280,268,284,2..., dimensions={0} | all-to-all | bytes 131072 | tf_op jit(solution)/shard_map/all_to_all | solution.py:490
  47.9 0.0 copy-done.2
  47.9 0.0 copy-done.3
  47.9 0.4 update.1
  48.3 15.5 %all_to_all.22 = bf16[32,4,128]{2,1,0:T(4,128)(2,1)S(1)} all-to-all(bf16[32,4,128]{2,1,0:T(4,128)(2,1)S(1)} %bitcast.21), channel_id=1, replica_groups={{8,24,12,28,0,16,4,20,136,152,140,156,128,144,132,148,264,280,268,284,2..., dimensions={0} | all-to-all | bytes 65536 | tf_op jit(solution)/shard_map/all_to_all | solution.py:503
  63.8 0.1 broadcast_in_dim.8
  63.9 14.0 %all_to_all.23 = bf16[16,128,128]{2,1,0:T(8,128)(2,1)S(1)} all-to-all(bf16[16,128,128]{2,1,0:T(8,128)(2,1)S(1)} %broadcast_in_dim.8), channel_id=1, replica_groups={{66,98,2,34,67,99,3,35,64,96,0,32,65,97,1,33},{70,102,6,38,71,103,7,39,..., dimensions={0} | all-to-all | bytes 1048576 | tf_op jit(solution)/shard_map/all_to_all | solution.py:512
  77.9 2.4 %collective-permute-start.1 = (bf16[2048,128]{1,0:T(8,128)(2,1)S(1)}, bf16[2048,128]{1,0:T(8,128)(2,1)S(1)}, u32[]{:S(2)}, u32[]{:S(2)}) collective-permute-start(bf16[2048,128]{1,0:T(8,128)(2,1)S(1)} %bitcast.13), channel_id=1, source_target_pairs={{0,16},{16,0},{1,17},{17,1},{2,18},{18,2},{3,19},{19,3},{4,20},{20... | collective-permute-start | bytes 1572872 | tf_op jit(solution)/shard_map/ppermute | solution.py:513
  80.3 0.0 copy-done
  80.3 0.0 copy-done.1
  80.3 1.9 %expand_own.1.part_ref = f32[512,1024]{1,0:T(8,128)S(1)} custom-call(bf16[2048,128]{1,0:T(8,128)(2,1)S(1)} %bitcast.14, bf16[512,1024]{1,0:T(8,128)(2,1)S(1)} %get-tuple-element.15.slope_ref, bf16[256,256]{1,0:T(8,128)(2,1)S(1)} %get-tuple-element.20.l_ref, bf16[2,256,1024]{2,1,0:T(8,128)(2,1)S(1)} %copy-done.1, bf16[2,256,1024]{2,1,0:T(8,128)(2,1)S(1)} %copy-done, ...), custom_call_target="tpu_custom_call" | custom-call | flops 3000000000 | bytes 4194304 | tf_op jit(solution)/shard_map/expand_own/pallas_call | solution.py:516
  82.2 0.0 collective-permute-done.1.modes_ref
  82.3 2.7 %expand.1 = (f32[512,1024]{1,0:T(8,128)}, f32[2,8192]{1,0:T(2,128)}) custom-call(bf16[2048,128]{1,0:T(8,128)(2,1)S(1)} %collective-permute-done.1.modes_ref, f32[512,1024]{1,0:T(8,128)S(1)} %expand_own.1.part_ref, bf16[2,256,1024]{2,1,0:T(8,128)(2,1)S(1)} %copy-done.1, bf16[2,256,1024]{2,1,0:T(8,128)(2,1)S(1)} %copy-done, ...), custom_call_target="tpu_custom_call" | custom-call | bytes 4194304 | tf_op jit(solution)/shard_map/expand/pallas_call | solution.py:525
  (1 shorter events, 0.0 us)
Async XLA Ops:
  0.6 11.4 %copy-start.4 = (bf16[16,16]{1,0:T(8,128)(2,1)S(1)}, bf16[16,16]{1,0:T(8,128)(2,1)}, u32[]{:S(2)}) copy-start(bf16[16,16]{1,0:T(8,128)(2,1)} %local_ref.1) | copy-start | bytes 1540
  3.2 10.6 %collective-permute-start = (f32[512,256]{1,0:T(8,128)S(1)}, f32[512,256]{1,0:T(8,128)S(1)}, u32[]{:S(2)}, u32[]{:S(2)}) collective-permute-start(f32[512,256]{1,0:T(8,128)S(1)} %get-tuple-element.14), channel_id=1, source_target_pairs={{0,16},{16,0},{1,17},{17,1},{2,18},{18,2},{3,19},{19,3},{4,20},{20... | collective-permute-start | bytes 1572872 | tf_op jit(solution)/shard_map/ppermute | solution.py:463
  13.8 34.0 %copy-start.2 = (f32[1,2,8192]{2,1,0:T(2,128)S(1)}, f32[1,2,8192]{2,1,0:T(2,128)}, u32[]{:S(2)}) copy-start(f32[1,2,8192]{2,1,0:T(2,128)} %param.10) | copy-start | bytes 196612
  13.9 34.0 %copy-start.3 = (f32[1,2,512]{2,1,0:T(2,128)S(1)}, f32[1,2,512]{2,1,0:T(2,128)}, u32[]{:S(2)}) copy-start(f32[1,2,512]{2,1,0:T(2,128)} %param.9) | copy-start | bytes 12292
  14.8 65.5 %copy-start = (bf16[2,256,1024]{2,1,0:T(8,128)(2,1)S(1)}, bf16[2,256,1024]{2,1,0:T(8,128)(2,1)}, u32[]{:S(2)}) copy-start(bf16[2,256,1024]{2,1,0:T(8,128)(2,1)} %constant.7.clone.low_ref) | copy-start | bytes 3145732
  14.8 65.5 %copy-start.1 = (bf16[2,256,1024]{2,1,0:T(8,128)(2,1)S(1)}, bf16[2,256,1024]{2,1,0:T(8,128)(2,1)}, u32[]{:S(2)}) copy-start(bf16[2,256,1024]{2,1,0:T(8,128)(2,1)} %constant.6.clone.high_ref) | copy-start | bytes 3145732
  77.9 4.3 %collective-permute-start.1 = (bf16[2048,128]{1,0:T(8,128)(2,1)S(1)}, bf16[2048,128]{1,0:T(8,128)(2,1)S(1)}, u32[]{:S(2)}, u32[]{:S(2)}) collective-permute-start(bf16[2048,128]{1,0:T(8,128)(2,1)S(1)} %bitcast.13), channel_id=1, source_target_pairs={{0,16},{16,0},{1,17},{17,1},{2,18},{18,2},{3,19},{19,3},{4,20},{20... | collective-permute-start | bytes 1572872 | tf_op jit(solution)/shard_map/ppermute | solution.py:513

commit v5 on v4

--- a/solution.py
+++ b/solution.py
@@ -43,10 +43,9 @@
     expand = np.stack([np.cos(depth_angle).T, -np.sin(depth_angle).T], 0) * NORM
     expand = expand.reshape(2, 2, 8, DEPTH).transpose(1, 0, 2, 3).reshape(2, KZ, DEPTH)
     expand = np.stack([np.kron(part, np.eye(CH)) for part in expand])
-    expand_high, expand_low = split_table(expand)
+    expand = np.stack(split_table(expand), 1)
     return dict(
-        expand_high=expand_high,
-        expand_low=expand_low,
+        expand=expand,
     )
 
 
@@ -289,8 +288,12 @@
         out_ref[y * BLOCK : (y + 1) * BLOCK, :] = turned[:, lanes_of(y)].astype(BF16)
 
 
+def sum_kernel(part_ref, out_ref):
+    out_ref[...] = jnp.sum(part_ref[...].astype(F32), 0).astype(BF16)
+
+
 def update_kernel(sum_ref, spectra_ref, weight_ref, gw_ref, sg_ref):
-    halves = [jnp.sum(sum_ref[:, half], 0) * NORM for half in range(2)]
+    halves = [jnp.sum(sum_ref[:, half].astype(F32), 0) * NORM for half in range(2)]
     grad = jnp.concatenate([halves[0][:2], halves[1][:2], halves[0][2:], halves[1][2:]], 0)
     saved = jnp.concatenate([spectra_ref[:, b * 128 : (b + 1) * 128] for b in range(4)], 0)
     shape = (64, QUARTER)
@@ -362,18 +365,18 @@
 
 
 def expand_own_kernel(
-    modes_ref, slope_ref, l_ref, high_ref, low_ref, x_ref, iy_ref, out_ref, wide_ref, rhs_ref
+    modes_ref, slope_ref, l_ref, depth_ref, x_ref, iy_ref, out_ref, wide_ref, rhs_ref
 ):
     turn_back(modes_ref, wide_ref)
     high, low = cells_of(0, TILE_X, x_ref, iy_ref, wide_ref, rhs_ref)
     half = lax.axis_index("c")
     for part in range(4):
         lanes = slice(part * 256, (part + 1) * 256)
-        table = high_ref[half, :, lanes]
+        table = depth_ref[half, 0, :, lanes]
         out_ref[:, lanes] = (
             dot(high, table)
             + dot(low, table)
-            + dot(high, low_ref[half, :, lanes])
+            + dot(high, depth_ref[half, 1, :, lanes])
             + dot(slope_ref[:, lanes], l_ref[...])
         )
 
@@ -381,8 +384,7 @@
 def expand_kernel(
     modes_ref,
     part_ref,
-    high_ref,
-    low_ref,
+    depth_ref,
     x_ref,
     iy_ref,
     gw_ref,
@@ -402,11 +404,11 @@
     high, low = cells_of(0, TILE_X, x_ref, iy_ref, wide_ref, rhs_ref)
     for part in range(4):
         lanes = slice(part * 256, (part + 1) * 256)
-        table = high_ref[half, :, lanes]
+        table = depth_ref[half, 0, :, lanes]
         out_ref[:, lanes] = (
             dot(high, table)
             + dot(low, table)
-            + dot(high, low_ref[half, :, lanes])
+            + dot(high, depth_ref[half, 1, :, lanes])
             + part_ref[:, lanes]
         )
         copy = pltpu.make_async_copy(out_ref.at[:, lanes], out_hbm.at[:, lanes], sems.at[part])
@@ -486,7 +488,15 @@
         [turn_scratch, *cell_scratch],
     )(depth, own, forward_x, forward_y)
     partial = lax.all_to_all(partial.reshape(16, 128, QUARTER), PLANE, 0, 0, tiled=True, axis_index_groups=PLANE_ORDER)
-    sums = jnp.sum(partial.astype(F32), 0).reshape(32, 4, QUARTER)
+    (sums,) = call(
+        sum_kernel,
+        "sums",
+        [((128, QUARTER), BF16)],
+        in_vmem(1),
+        in_vmem(1),
+        [],
+    )(partial)
+    sums = sums.reshape(32, 4, QUARTER)
     sums = lax.all_to_all(sums, LINE, 0, 0, tiled=True, axis_index_groups=LINE_ORDER)
     grad_weight, back = call(
         update_kernel,
@@ -512,21 +522,20 @@
     modes = lax.all_to_all(back, PLANE, 0, 0, tiled=True, axis_index_groups=PLANE_ORDER).reshape(2048, QUARTER)
     other = lax.ppermute(modes, "c", swap)
     back_scratch = [pltpu.VMEM((BLOCK, YS * QUARTER), BF16), turn_scratch]
-    depth_tables = (table["expand_high"], table["expand_low"])
     (part,) = call(
         expand_own_kernel,
         "expand_own",
         [((ROWS, ROW), F32)],
-        in_vmem(7),
+        in_vmem(6),
         in_vmem(1),
         back_scratch,
         flops=3 * 10**9,
-    )(modes, slope, local_map, *depth_tables, inverse_x, inverse_y)
+    )(modes, slope, local_map, table["expand"], inverse_x, inverse_y)
     result, grad_weight = call(
         expand_kernel,
         "expand",
         [((ROWS, ROW), F32), ((2, 8192), F32)],
-        in_vmem(7),
+        in_vmem(6),
         [IN_HBM, IN_HBM],
         [
             *back_scratch,
@@ -534,7 +543,7 @@
             pltpu.SemaphoreType.DMA((4,)),
             pltpu.SemaphoreType.DMA,
         ],
-    )(other, part, *depth_tables, inverse_x, inverse_y, grad_weight)
+    )(other, part, table["expand"], inverse_x, inverse_y, grad_weight)
     return result.reshape(TILE_X, TILE_Y, ROW), grad_weight.reshape(1, 2, 8192)
 
 

time: 85.3 us -> 84.2 us (0.987)
  blocking collectives: 62.4 us -> 61.4 us
    all_to_all x1, blocking collectives: 19.1 us -> 18 us  [on_device(): lax.all_to_all(sums, LINE, 0, 0, tiled=True, axis_index_groups=LINE_ORDER)]
    pallas_call x1 -> x2, Pallas kernels: 1.89 us -> 1.97 us  [the longest x1 1.89 us: on_device(): call(expand_own_kernel, 'expand_own', [((ROWS, ROW), F32)], in_vmem(6), i...]
where the time goes in v5:
time: 84.2 us; the launch traced here: 83.9 us
  blocking collectives  61.4 us (73%)
  starting transfers between devices  11.2 us (13%)
  Pallas kernels  10.4 us (12%)
    all_to_all x1, blocking collectives, on_device(): lax.all_to_all(sums, LINE, 0, 0, tiled=True, axis_index_groups=LINE_ORDER)  18 us
    all_to_all x1, blocking collectives, on_device(): lax.all_to_all(back.reshape(32, 4, QUARTER).astype(BF16), LINE, 0, 0, til...  15.5 us
    all_to_all x1, blocking collectives, on_device(): lax.all_to_all(back, PLANE, 0, 0, tiled=True, axis_index_groups=PLANE_ORDER)  14 us
    all_to_all x1, blocking collectives, on_device(): lax.all_to_all(partial.reshape(16, 128, QUARTER), PLANE, 0, 0, tiled=True...  13.9 us
    ppermute x1, starting transfers between devices, on_device(): depth = lax.ppermute(send, 'c', swap)  8.79 us
    pallas_call x1, Pallas kernels, on_device(): call(expand_kernel, 'expand', [((ROWS, ROW), F32), ((2, 8192), F32)], in_...  2.72 us
    pallas_call x1, Pallas kernels, on_device(): call(slope_kernel, 'slope', [((ROWS, ROW), BF16), (square, F32)], [IN_HBM...  2.54 us
    ppermute x1, starting transfers between devices, on_device(): other = lax.ppermute(modes, 'c', swap)  2.39 us
  transfers between devices with their start and end apart: 2, of which 0 were waited for; matrix products, arithmetic and copies ran while one was open for 0% of the time, Pallas kernels for 4%

profile of v5, /device:TPU:1, one launch (start us, length us, event | category | flops | bytes accessed | tf_op | source)
XLA Modules:
  0.0 83.9 jit_solution(6689755594825769807)
XLA Ops:
  0.6 0.0 copy-start.3
  0.6 2.5 %slope.1 = (bf16[512,1024]{1,0:T(8,128)(2,1)S(1)}, f32[512,256]{1,0:T(8,128)S(1)}) custom-call(bf16[512,1024]{1,0:T(8,128)(2,1)} %bitcast.19, bf16[512,1024]{1,0:T(8,128)(2,1)} %bitcast.20), custom_call_target="tpu_custom_call" | custom-call | bytes 4194304 | tf_op jit(solution)/shard_map/slope/pallas_call | solution.py:452
  3.2 8.8 %collective-permute-start = (f32[512,256]{1,0:T(8,128)S(1)}, f32[512,256]{1,0:T(8,128)S(1)}, u32[]{:S(2)}, u32[]{:S(2)}) collective-permute-start(f32[512,256]{1,0:T(8,128)S(1)} %get-tuple-element.14), channel_id=1, source_target_pairs={{0,16},{16,0},{1,17},{17,1},{2,18},{18,2},{3,19},{19,3},{4,20},{20... | collective-permute-start | bytes 1572872 | tf_op jit(solution)/shard_map/ppermute | solution.py:465
  12.0 0.0 copy-done.3
  12.0 1.8 %own_cells.1 = (f32[512,512]{1,0:T(8,128)S(1)}, bf16[2,2,512,256]{3,2,1,0:T(8,128)(2,1)S(1)}, bf16[2,256,512]{2,1,0:T(8,128)(2,1)S(1)}, bf16[256,256]{1,0:T(8,12...) custom-call(bf16[512,1024]{1,0:T(8,128)(2,1)S(1)} %get-tuple-element.15.slope_ref, ...), custom_call_target="tpu_custom_call" | custom-call | flops 2000000000 | bytes 4194304 | tf_op jit(solution)/shard_map/own_cells/pallas_call | solution.py:466
  13.8 0.0 collective-permute-done.depth_ref
  13.8 0.0 copy-start.1
  13.9 0.0 copy-start.2
  13.9 0.9 %modes.1 = bf16[2048,128]{1,0:T(8,128)(2,1)S(1)} custom-call(f32[512,256]{1,0:T(8,128)S(1)} %collective-permute-done.depth_ref, f32[512,512]{1,0:T(8,128)S(1)} %get-tuple-element.16.part_ref, bf16[2,2,512,256]{3,2,1,0:T(8,128)(2,1)S(1)} %get-tuple-element.17.x_ref, bf16[64,192]{1,0:T(8,128)(2,1)S(1)} %get-tuple-element.18.fy_ref), custom_call_target="tpu_custom_call" | custom-call | bytes 4194304 | tf_op jit(solution)/shard_map/modes/pallas_call | solution.py:482
  14.8 0.0 copy-start
  14.8 13.9 %all_to_all.20.part_ref = bf16[16,128,128]{2,1,0:T(8,128)(2,1)S(1)} all-to-all(bf16[16,128,128]{2,1,0:T(8,128)(2,1)S(1)} %bitcast.12), channel_id=1, replica_groups={{66,98,2,34,67,99,3,35,64,96,0,32,65,97,1,33},{70,102,6,38,71,103,7,39,..., dimensions={0} | all-to-all | bytes 1048576 | tf_op jit(solution)/shard_map/all_to_all | solution.py:490
  28.7 0.1 sums.1
  28.8 18.0 %all_to_all.21 = bf16[32,4,128]{2,1,0:T(4,128)(2,1)S(1)} all-to-all(bf16[32,4,128]{2,1,0:T(4,128)(2,1)S(1)} %bitcast.16), channel_id=1, replica_groups={{8,24,12,28,0,16,4,20,136,152,140,156,128,144,132,148,264,280,268,284,2..., dimensions={0} | all-to-all | bytes 65536 | tf_op jit(solution)/shard_map/all_to_all | solution.py:500
  46.7 0.0 copy-done.1
  46.8 0.0 copy-done.2
  46.8 0.4 update.1
  47.2 15.5 %all_to_all.22 = bf16[32,4,128]{2,1,0:T(4,128)(2,1)S(1)} all-to-all(bf16[32,4,128]{2,1,0:T(4,128)(2,1)S(1)} %bitcast.21), channel_id=1, replica_groups={{8,24,12,28,0,16,4,20,136,152,140,156,128,144,132,148,264,280,268,284,2..., dimensions={0} | all-to-all | bytes 65536 | tf_op jit(solution)/shard_map/all_to_all | solution.py:513
  62.8 0.1 broadcast_in_dim.8
  62.9 14.0 %all_to_all.23 = bf16[16,128,128]{2,1,0:T(8,128)(2,1)S(1)} all-to-all(bf16[16,128,128]{2,1,0:T(8,128)(2,1)S(1)} %broadcast_in_dim.8), channel_id=1, replica_groups={{66,98,2,34,67,99,3,35,64,96,0,32,65,97,1,33},{70,102,6,38,71,103,7,39,..., dimensions={0} | all-to-all | bytes 1048576 | tf_op jit(solution)/shard_map/all_to_all | solution.py:522
  76.9 2.4 %collective-permute-start.1 = (bf16[2048,128]{1,0:T(8,128)(2,1)S(1)}, bf16[2048,128]{1,0:T(8,128)(2,1)S(1)}, u32[]{:S(2)}, u32[]{:S(2)}) collective-permute-start(bf16[2048,128]{1,0:T(8,128)(2,1)S(1)} %bitcast.13), channel_id=1, source_target_pairs={{0,16},{16,0},{1,17},{17,1},{2,18},{18,2},{3,19},{19,3},{4,20},{20... | collective-permute-start | bytes 1572872 | tf_op jit(solution)/shard_map/ppermute | solution.py:523
  79.3 0.0 copy-done
  79.3 1.9 %expand_own.1.part_ref = f32[512,1024]{1,0:T(8,128)S(1)} custom-call(bf16[2048,128]{1,0:T(8,128)(2,1)S(1)} %bitcast.14, bf16[512,1024]{1,0:T(8,128)(2,1)S(1)} %get-tuple-element.15.slope_ref, bf16[256,256]{1,0:T(8,128)(2,1)S(1)} %get-tuple-element.20.l_ref, bf16[2,2,256,1024]{3,2,1,0:T(8,128)(2,1)S(1)} %copy-done, ...), custom_call_target="tpu_custom_call" | custom-call | flops 3000000000 | bytes 4194304 | tf_op jit(solution)/shard_map/expand_own/pallas_call | solution.py:525
  81.2 0.0 collective-permute-done.1.modes_ref
  81.2 2.7 %expand.1 = (f32[512,1024]{1,0:T(8,128)}, f32[2,8192]{1,0:T(2,128)}) custom-call(bf16[2048,128]{1,0:T(8,128)(2,1)S(1)} %collective-permute-done.1.modes_ref, f32[512,1024]{1,0:T(8,128)S(1)} %expand_own.1.part_ref, bf16[2,2,256,1024]{3,2,1,0:T(8,128)(2,1)S(1)} %copy-done, bf16[2,256,512]{2,1,0:T(8,128)(2,1)S(1)} %get-tuple-element.21.x_ref, ...), custom_call_target="tpu_custom_call" | custom-call | bytes 4194304 | tf_op jit(solution)/shard_map/expand/pallas_call | solution.py:534
  (1 shorter events, 0.0 us)
Async XLA Ops:
  0.6 11.4 %copy-start.3 = (bf16[16,16]{1,0:T(8,128)(2,1)S(1)}, bf16[16,16]{1,0:T(8,128)(2,1)}, u32[]{:S(2)}) copy-start(bf16[16,16]{1,0:T(8,128)(2,1)} %local_ref.1) | copy-start | bytes 1540
  3.2 10.6 %collective-permute-start = (f32[512,256]{1,0:T(8,128)S(1)}, f32[512,256]{1,0:T(8,128)S(1)}, u32[]{:S(2)}, u32[]{:S(2)}) collective-permute-start(f32[512,256]{1,0:T(8,128)S(1)} %get-tuple-element.14), channel_id=1, source_target_pairs={{0,16},{16,0},{1,17},{17,1},{2,18},{18,2},{3,19},{19,3},{4,20},{20... | collective-permute-start | bytes 1572872 | tf_op jit(solution)/shard_map/ppermute | solution.py:465
  13.8 32.9 %copy-start.1 = (f32[1,2,8192]{2,1,0:T(2,128)S(1)}, f32[1,2,8192]{2,1,0:T(2,128)}, u32[]{:S(2)}) copy-start(f32[1,2,8192]{2,1,0:T(2,128)} %param.9) | copy-start | bytes 196612
  13.9 32.9 %copy-start.2 = (f32[1,2,512]{2,1,0:T(2,128)S(1)}, f32[1,2,512]{2,1,0:T(2,128)}, u32[]{:S(2)}) copy-start(f32[1,2,512]{2,1,0:T(2,128)} %param.8) | copy-start | bytes 12292
  14.8 64.4 %copy-start = (bf16[2,2,256,1024]{3,2,1,0:T(8,128)(2,1)S(1)}, bf16[2,2,256,1024]{3,2,1,0:T(8,128)(2,1)}, u32[]{:S(2)}) copy-start(bf16[2,2,256,1024]{3,2,1,0:T(8,128)(2,1)} %constant.2.clone.depth_ref) | copy-start | bytes 6291460
  76.9 4.3 %collective-permute-start.1 = (bf16[2048,128]{1,0:T(8,128)(2,1)S(1)}, bf16[2048,128]{1,0:T(8,128)(2,1)S(1)}, u32[]{:S(2)}, u32[]{:S(2)}) collective-permute-start(bf16[2048,128]{1,0:T(8,128)(2,1)S(1)} %bitcast.13), channel_id=1, source_target_pairs={{0,16},{16,0},{1,17},{17,1},{2,18},{18,2},{3,19},{19,3},{4,20},{20... | collective-permute-start | bytes 1572872 | tf_op jit(solution)/shard_map/ppermute | solution.py:523

commit v6 on v5

--- a/solution.py
+++ b/solution.py
@@ -227,7 +227,7 @@
         pre_value = pre_ref[rows, :].astype(F32)
         slope = (cot_ref[rows, :].astype(F32) * gelu_slope(pre_value)).astype(BF16)
         slope_ref[rows, :] = slope
-        send_ref[rows, :] = dot(slope_ref[rows, :], f_ref[...])
+    send_ref[...] = dot(slope_ref[...], f_ref[...])
 
 
 def turn_y(depth, fy_ref, rhs_ref, high_ref, low_ref):

time: 84.2 us -> 84.2 us (level)
  no operation moved by 1% of the time
where the time goes in v6:
time: 84.2 us; the launch traced here: 83.9 us
  blocking collectives  61.4 us (73%)
  starting transfers between devices  11.2 us (13%)
  Pallas kernels  10.4 us (12%)
    all_to_all x1, blocking collectives, on_device(): lax.all_to_all(sums, LINE, 0, 0, tiled=True, axis_index_groups=LINE_ORDER)  18 us
    all_to_all x1, blocking collectives, on_device(): lax.all_to_all(back.reshape(32, 4, QUARTER).astype(BF16), LINE, 0, 0, til...  15.5 us
    all_to_all x1, blocking collectives, on_device(): lax.all_to_all(back, PLANE, 0, 0, tiled=True, axis_index_groups=PLANE_ORDER)  14 us
    all_to_all x1, blocking collectives, on_device(): lax.all_to_all(partial.reshape(16, 128, QUARTER), PLANE, 0, 0, tiled=True...  13.9 us
    ppermute x1, starting transfers between devices, on_device(): depth = lax.ppermute(send, 'c', swap)  8.79 us
    pallas_call x1, Pallas kernels, on_device(): call(expand_kernel, 'expand', [((ROWS, ROW), F32), ((2, 8192), F32)], in_...  2.73 us
    pallas_call x1, Pallas kernels, on_device(): call(slope_kernel, 'slope', [((ROWS, ROW), BF16), (square, F32)], [IN_HBM...  2.48 us
    ppermute x1, starting transfers between devices, on_device(): other = lax.ppermute(modes, 'c', swap)  2.39 us
  transfers between devices with their start and end apart: 2, of which 0 were waited for; matrix products, arithmetic and copies ran while one was open for 0% of the time, Pallas kernels for 4%

profile of v6, /device:TPU:1, one launch (start us, length us, event | category | flops | bytes accessed | tf_op | source)
XLA Modules:
  0.0 83.9 jit_solution(11534748967273433186)
XLA Ops:
  0.6 0.0 copy-start.3
  0.6 2.5 %slope.1 = (bf16[512,1024]{1,0:T(8,128)(2,1)S(1)}, f32[512,256]{1,0:T(8,128)S(1)}) custom-call(bf16[512,1024]{1,0:T(8,128)(2,1)} %bitcast.19, bf16[512,1024]{1,0:T(8,128)(2,1)} %bitcast.20), custom_call_target="tpu_custom_call" | custom-call | bytes 4194304 | tf_op jit(solution)/shard_map/slope/pallas_call | solution.py:452
  3.1 8.8 %collective-permute-start = (f32[512,256]{1,0:T(8,128)S(1)}, f32[512,256]{1,0:T(8,128)S(1)}, u32[]{:S(2)}, u32[]{:S(2)}) collective-permute-start(f32[512,256]{1,0:T(8,128)S(1)} %get-tuple-element.14), channel_id=1, source_target_pairs={{0,16},{16,0},{1,17},{17,1},{2,18},{18,2},{3,19},{19,3},{4,20},{20... | collective-permute-start | bytes 1572872 | tf_op jit(solution)/shard_map/ppermute | solution.py:465
  11.9 0.0 copy-done.3
  11.9 1.8 %own_cells.1 = (f32[512,512]{1,0:T(8,128)S(1)}, bf16[2,2,512,256]{3,2,1,0:T(8,128)(2,1)S(1)}, bf16[2,256,512]{2,1,0:T(8,128)(2,1)S(1)}, bf16[256,256]{1,0:T(8,12...) custom-call(bf16[512,1024]{1,0:T(8,128)(2,1)S(1)} %get-tuple-element.15.slope_ref, ...), custom_call_target="tpu_custom_call" | custom-call | flops 2000000000 | bytes 4194304 | tf_op jit(solution)/shard_map/own_cells/pallas_call | solution.py:466
  13.8 0.0 collective-permute-done.depth_ref
  13.8 0.0 copy-start.1
  13.8 0.0 copy-start.2
  13.8 0.9 %modes.1 = bf16[2048,128]{1,0:T(8,128)(2,1)S(1)} custom-call(f32[512,256]{1,0:T(8,128)S(1)} %collective-permute-done.depth_ref, f32[512,512]{1,0:T(8,128)S(1)} %get-tuple-element.16.part_ref, bf16[2,2,512,256]{3,2,1,0:T(8,128)(2,1)S(1)} %get-tuple-element.17.x_ref, bf16[64,192]{1,0:T(8,128)(2,1)S(1)} %get-tuple-element.18.fy_ref), custom_call_target="tpu_custom_call" | custom-call | bytes 4194304 | tf_op jit(solution)/shard_map/modes/pallas_call | solution.py:482
  14.8 0.0 copy-start
  14.8 13.9 %all_to_all.20.part_ref = bf16[16,128,128]{2,1,0:T(8,128)(2,1)S(1)} all-to-all(bf16[16,128,128]{2,1,0:T(8,128)(2,1)S(1)} %bitcast.12), channel_id=1, replica_groups={{66,98,2,34,67,99,3,35,64,96,0,32,65,97,1,33},{70,102,6,38,71,103,7,39,..., dimensions={0} | all-to-all | bytes 1048576 | tf_op jit(solution)/shard_map/all_to_all | solution.py:490
  28.6 0.1 sums.1
  28.7 18.0 %all_to_all.21 = bf16[32,4,128]{2,1,0:T(4,128)(2,1)S(1)} all-to-all(bf16[32,4,128]{2,1,0:T(4,128)(2,1)S(1)} %bitcast.16), channel_id=1, replica_groups={{8,24,12,28,0,16,4,20,136,152,140,156,128,144,132,148,264,280,268,284,2..., dimensions={0} | all-to-all | bytes 65536 | tf_op jit(solution)/shard_map/all_to_all | solution.py:500
  46.7 0.0 copy-done.1
  46.7 0.0 copy-done.2
  46.7 0.4 update.1
  47.2 15.5 %all_to_all.22 = bf16[32,4,128]{2,1,0:T(4,128)(2,1)S(1)} all-to-all(bf16[32,4,128]{2,1,0:T(4,128)(2,1)S(1)} %bitcast.21), channel_id=1, replica_groups={{8,24,12,28,0,16,4,20,136,152,140,156,128,144,132,148,264,280,268,284,2..., dimensions={0} | all-to-all | bytes 65536 | tf_op jit(solution)/shard_map/all_to_all | solution.py:513
  62.7 0.1 broadcast_in_dim.8
  62.8 14.0 %all_to_all.23 = bf16[16,128,128]{2,1,0:T(8,128)(2,1)S(1)} all-to-all(bf16[16,128,128]{2,1,0:T(8,128)(2,1)S(1)} %broadcast_in_dim.8), channel_id=1, replica_groups={{66,98,2,34,67,99,3,35,64,96,0,32,65,97,1,33},{70,102,6,38,71,103,7,39,..., dimensions={0} | all-to-all | bytes 1048576 | tf_op jit(solution)/shard_map/all_to_all | solution.py:522
  76.8 2.4 %collective-permute-start.1 = (bf16[2048,128]{1,0:T(8,128)(2,1)S(1)}, bf16[2048,128]{1,0:T(8,128)(2,1)S(1)}, u32[]{:S(2)}, u32[]{:S(2)}) collective-permute-start(bf16[2048,128]{1,0:T(8,128)(2,1)S(1)} %bitcast.13), channel_id=1, source_target_pairs={{0,16},{16,0},{1,17},{17,1},{2,18},{18,2},{3,19},{19,3},{4,20},{20... | collective-permute-start | bytes 1572872 | tf_op jit(solution)/shard_map/ppermute | solution.py:523
  79.2 0.0 copy-done
  79.2 1.9 %expand_own.1.part_ref = f32[512,1024]{1,0:T(8,128)S(1)} custom-call(bf16[2048,128]{1,0:T(8,128)(2,1)S(1)} %bitcast.14, bf16[512,1024]{1,0:T(8,128)(2,1)S(1)} %get-tuple-element.15.slope_ref, bf16[256,256]{1,0:T(8,128)(2,1)S(1)} %get-tuple-element.20.l_ref, bf16[2,2,256,1024]{3,2,1,0:T(8,128)(2,1)S(1)} %copy-done, ...), custom_call_target="tpu_custom_call" | custom-call | flops 3000000000 | bytes 4194304 | tf_op jit(solution)/shard_map/expand_own/pallas_call | solution.py:525
  81.1 0.0 collective-permute-done.1.modes_ref
  81.1 2.7 %expand.1 = (f32[512,1024]{1,0:T(8,128)}, f32[2,8192]{1,0:T(2,128)}) custom-call(bf16[2048,128]{1,0:T(8,128)(2,1)S(1)} %collective-permute-done.1.modes_ref, f32[512,1024]{1,0:T(8,128)S(1)} %expand_own.1.part_ref, bf16[2,2,256,1024]{3,2,1,0:T(8,128)(2,1)S(1)} %copy-done, bf16[2,256,512]{2,1,0:T(8,128)(2,1)S(1)} %get-tuple-element.21.x_ref, ...), custom_call_target="tpu_custom_call" | custom-call | bytes 4194304 | tf_op jit(solution)/shard_map/expand/pallas_call | solution.py:534
  (1 shorter events, 0.0 us)
Async XLA Ops:
  0.6 11.3 %copy-start.3 = (bf16[16,16]{1,0:T(8,128)(2,1)S(1)}, bf16[16,16]{1,0:T(8,128)(2,1)}, u32[]{:S(2)}) copy-start(bf16[16,16]{1,0:T(8,128)(2,1)} %local_ref.1) | copy-start | bytes 1540
  3.1 10.7 %collective-permute-start = (f32[512,256]{1,0:T(8,128)S(1)}, f32[512,256]{1,0:T(8,128)S(1)}, u32[]{:S(2)}, u32[]{:S(2)}) collective-permute-start(f32[512,256]{1,0:T(8,128)S(1)} %get-tuple-element.14), channel_id=1, source_target_pairs={{0,16},{16,0},{1,17},{17,1},{2,18},{18,2},{3,19},{19,3},{4,20},{20... | collective-permute-start | bytes 1572872 | tf_op jit(solution)/shard_map/ppermute | solution.py:465
  13.8 32.9 %copy-start.1 = (f32[1,2,8192]{2,1,0:T(2,128)S(1)}, f32[1,2,8192]{2,1,0:T(2,128)}, u32[]{:S(2)}) copy-start(f32[1,2,8192]{2,1,0:T(2,128)} %param.9) | copy-start | bytes 196612
  13.8 32.9 %copy-start.2 = (f32[1,2,512]{2,1,0:T(2,128)S(1)}, f32[1,2,512]{2,1,0:T(2,128)}, u32[]{:S(2)}) copy-start(f32[1,2,512]{2,1,0:T(2,128)} %param.8) | copy-start | bytes 12292
  14.8 64.5 %copy-start = (bf16[2,2,256,1024]{3,2,1,0:T(8,128)(2,1)S(1)}, bf16[2,2,256,1024]{3,2,1,0:T(8,128)(2,1)}, u32[]{:S(2)}) copy-start(bf16[2,2,256,1024]{3,2,1,0:T(8,128)(2,1)} %constant.2.clone.depth_ref) | copy-start | bytes 6291460
  76.8 4.3 %collective-permute-start.1 = (bf16[2048,128]{1,0:T(8,128)(2,1)S(1)}, bf16[2048,128]{1,0:T(8,128)(2,1)S(1)}, u32[]{:S(2)}, u32[]{:S(2)}) collective-permute-start(bf16[2048,128]{1,0:T(8,128)(2,1)S(1)} %bitcast.13), channel_id=1, source_target_pairs={{0,16},{16,0},{1,17},{17,1},{2,18},{18,2},{3,19},{19,3},{4,20},{20... | collective-permute-start | bytes 1572872 | tf_op jit(solution)/shard_map/ppermute | solution.py:523

commit v7 on v5

--- a/solution.py
+++ b/solution.py
@@ -27,7 +27,7 @@
 PLANE = ("y", "x")
 LINE = ("zl", "zh", "c")
 FAR, FAR_PLANE = 2, 2
-LINE_ORDER = [[(zl * ZH + (zh ^ FAR)) * CS + c for zl in range(ZL) for zh in range(ZH) for c in range(CS)]]
+LINE_ORDER = [[((zl ^ 1) * ZH + (zh ^ FAR)) * CS + c for zl in range(ZL) for zh in range(ZH) for c in range(CS)]]
 PLANE_ORDER = [[(y ^ FAR_PLANE) * XS + (x ^ FAR_PLANE) for y in range(YS) for x in range(XS)]]
 
 
@@ -167,7 +167,7 @@
 def x_table(tile):
     shape = (2 * KX, 8 * TILE_X)
     row, column = iota(shape, 0), iota(shape, 1)
-    mode = mode_of((row >> 2 & 3) * 8 + ((row >> 4) ^ FAR_PLANE) * 2 + (row >> 1 & 1))
+    mode = mode_of(((row >> 2 & 3) ^ 1) * 8 + ((row >> 4) ^ FAR_PLANE) * 2 + (row >> 1 & 1))
     cell = (tile ^ (column >> 5 & 1)) * TILE_X + (column >> 1 & 15)
     value = turn(mode * cell + 128 * ((row & 1) - (column & 1)))
     high = value.astype(BF16)

time: 84.2 us -> 84.3 us (level)
  no operation moved by 1% of the time
where the time goes in v7:
time: 84.3 us; the launch traced here: 84 us
  blocking collectives  61.4 us (73%)
  starting transfers between devices  11.2 us (13%)
  Pallas kernels  10.4 us (12%)
    all_to_all x1, blocking collectives, on_device(): lax.all_to_all(sums, LINE, 0, 0, tiled=True, axis_index_groups=LINE_ORDER)  17.8 us
    all_to_all x1, blocking collectives, on_device(): lax.all_to_all(back.reshape(32, 4, QUARTER).astype(BF16), LINE, 0, 0, til...  15.8 us
    all_to_all x1, blocking collectives, on_device(): lax.all_to_all(back, PLANE, 0, 0, tiled=True, axis_index_groups=PLANE_ORDER)  14 us
    all_to_all x1, blocking collectives, on_device(): lax.all_to_all(partial.reshape(16, 128, QUARTER), PLANE, 0, 0, tiled=True...  13.9 us
    ppermute x1, starting transfers between devices, on_device(): depth = lax.ppermute(send, 'c', swap)  8.79 us
    pallas_call x1, Pallas kernels, on_device(): call(expand_kernel, 'expand', [((ROWS, ROW), F32), ((2, 8192), F32)], in_...  2.72 us
    pallas_call x1, Pallas kernels, on_device(): call(slope_kernel, 'slope', [((ROWS, ROW), BF16), (square, F32)], [IN_HBM...  2.54 us
    ppermute x1, starting transfers between devices, on_device(): other = lax.ppermute(modes, 'c', swap)  2.39 us
  transfers between devices with their start and end apart: 2, of which 0 were waited for; matrix products, arithmetic and copies ran while one was open for 0% of the time, Pallas kernels for 4%

profile of v7, /device:TPU:1, one launch (start us, length us, event | category | flops | bytes accessed | tf_op | source)
XLA Modules:
  0.0 84.0 jit_solution(3371844388629455186)
XLA Ops:
  0.6 0.0 copy-start.3
  0.6 2.5 %slope.1 = (bf16[512,1024]{1,0:T(8,128)(2,1)S(1)}, f32[512,256]{1,0:T(8,128)S(1)}) custom-call(bf16[512,1024]{1,0:T(8,128)(2,1)} %bitcast.19, bf16[512,1024]{1,0:T(8,128)(2,1)} %bitcast.20), custom_call_target="tpu_custom_call" | custom-call | bytes 4194304 | tf_op jit(solution)/shard_map/slope/pallas_call | solution.py:452
  3.2 8.8 %collective-permute-start = (f32[512,256]{1,0:T(8,128)S(1)}, f32[512,256]{1,0:T(8,128)S(1)}, u32[]{:S(2)}, u32[]{:S(2)}) collective-permute-start(f32[512,256]{1,0:T(8,128)S(1)} %get-tuple-element.14), channel_id=1, source_target_pairs={{0,16},{16,0},{1,17},{17,1},{2,18},{18,2},{3,19},{19,3},{4,20},{20... | collective-permute-start | bytes 1572872 | tf_op jit(solution)/shard_map/ppermute | solution.py:465
  12.0 0.0 copy-done.3
  12.0 1.8 %own_cells.1 = (f32[512,512]{1,0:T(8,128)S(1)}, bf16[2,2,512,256]{3,2,1,0:T(8,128)(2,1)S(1)}, bf16[2,256,512]{2,1,0:T(8,128)(2,1)S(1)}, bf16[256,256]{1,0:T(8,12...) custom-call(bf16[512,1024]{1,0:T(8,128)(2,1)S(1)} %get-tuple-element.15.slope_ref, ...), custom_call_target="tpu_custom_call" | custom-call | flops 2000000000 | bytes 4194304 | tf_op jit(solution)/shard_map/own_cells/pallas_call | solution.py:466
  13.8 0.0 collective-permute-done.depth_ref
  13.8 0.0 copy-start.1
  13.9 0.0 copy-start.2
  13.9 0.9 %modes.1 = bf16[2048,128]{1,0:T(8,128)(2,1)S(1)} custom-call(f32[512,256]{1,0:T(8,128)S(1)} %collective-permute-done.depth_ref, f32[512,512]{1,0:T(8,128)S(1)} %get-tuple-element.16.part_ref, bf16[2,2,512,256]{3,2,1,0:T(8,128)(2,1)S(1)} %get-tuple-element.17.x_ref, bf16[64,192]{1,0:T(8,128)(2,1)S(1)} %get-tuple-element.18.fy_ref), custom_call_target="tpu_custom_call" | custom-call | bytes 4194304 | tf_op jit(solution)/shard_map/modes/pallas_call | solution.py:482
  14.8 0.0 copy-start
  14.8 13.9 %all_to_all.20.part_ref = bf16[16,128,128]{2,1,0:T(8,128)(2,1)S(1)} all-to-all(bf16[16,128,128]{2,1,0:T(8,128)(2,1)S(1)} %bitcast.12), channel_id=1, replica_groups={{66,98,2,34,67,99,3,35,64,96,0,32,65,97,1,33},{70,102,6,38,71,103,7,39,..., dimensions={0} | all-to-all | bytes 1048576 | tf_op jit(solution)/shard_map/all_to_all | solution.py:490
  28.7 0.1 sums.1
  28.8 17.8 %all_to_all.21 = bf16[32,4,128]{2,1,0:T(4,128)(2,1)S(1)} all-to-all(bf16[32,4,128]{2,1,0:T(4,128)(2,1)S(1)} %bitcast.16), channel_id=1, replica_groups={{136,152,140,156,128,144,132,148,8,24,12,28,0,16,4,20,392,408,396,412,3..., dimensions={0} | all-to-all | bytes 65536 | tf_op jit(solution)/shard_map/all_to_all | solution.py:500
  46.6 0.0 copy-done.1
  46.6 0.0 copy-done.2
  46.6 0.4 update.1
  47.0 15.8 %all_to_all.22 = bf16[32,4,128]{2,1,0:T(4,128)(2,1)S(1)} all-to-all(bf16[32,4,128]{2,1,0:T(4,128)(2,1)S(1)} %bitcast.21), channel_id=1, replica_groups={{136,152,140,156,128,144,132,148,8,24,12,28,0,16,4,20,392,408,396,412,3..., dimensions={0} | all-to-all | bytes 65536 | tf_op jit(solution)/shard_map/all_to_all | solution.py:513
  62.8 0.1 broadcast_in_dim.8
  62.9 14.0 %all_to_all.23 = bf16[16,128,128]{2,1,0:T(8,128)(2,1)S(1)} all-to-all(bf16[16,128,128]{2,1,0:T(8,128)(2,1)S(1)} %broadcast_in_dim.8), channel_id=1, replica_groups={{66,98,2,34,67,99,3,35,64,96,0,32,65,97,1,33},{70,102,6,38,71,103,7,39,..., dimensions={0} | all-to-all | bytes 1048576 | tf_op jit(solution)/shard_map/all_to_all | solution.py:522
  76.9 2.4 %collective-permute-start.1 = (bf16[2048,128]{1,0:T(8,128)(2,1)S(1)}, bf16[2048,128]{1,0:T(8,128)(2,1)S(1)}, u32[]{:S(2)}, u32[]{:S(2)}) collective-permute-start(bf16[2048,128]{1,0:T(8,128)(2,1)S(1)} %bitcast.13), channel_id=1, source_target_pairs={{0,16},{16,0},{1,17},{17,1},{2,18},{18,2},{3,19},{19,3},{4,20},{20... | collective-permute-start | bytes 1572872 | tf_op jit(solution)/shard_map/ppermute | solution.py:523
  79.3 0.0 copy-done
  79.3 1.9 %expand_own.1.part_ref = f32[512,1024]{1,0:T(8,128)S(1)} custom-call(bf16[2048,128]{1,0:T(8,128)(2,1)S(1)} %bitcast.14, bf16[512,1024]{1,0:T(8,128)(2,1)S(1)} %get-tuple-element.15.slope_ref, bf16[256,256]{1,0:T(8,128)(2,1)S(1)} %get-tuple-element.20.l_ref, bf16[2,2,256,1024]{3,2,1,0:T(8,128)(2,1)S(1)} %copy-done, ...), custom_call_target="tpu_custom_call" | custom-call | flops 3000000000 | bytes 4194304 | tf_op jit(solution)/shard_map/expand_own/pallas_call | solution.py:525
  81.2 0.0 collective-permute-done.1.modes_ref
  81.2 2.7 %expand.1 = (f32[512,1024]{1,0:T(8,128)}, f32[2,8192]{1,0:T(2,128)}) custom-call(bf16[2048,128]{1,0:T(8,128)(2,1)S(1)} %collective-permute-done.1.modes_ref, f32[512,1024]{1,0:T(8,128)S(1)} %expand_own.1.part_ref, bf16[2,2,256,1024]{3,2,1,0:T(8,128)(2,1)S(1)} %copy-done, bf16[2,256,512]{2,1,0:T(8,128)(2,1)S(1)} %get-tuple-element.21.x_ref, ...), custom_call_target="tpu_custom_call" | custom-call | bytes 4194304 | tf_op jit(solution)/shard_map/expand/pallas_call | solution.py:534
  (1 shorter events, 0.0 us)
Async XLA Ops:
  0.6 11.4 %copy-start.3 = (bf16[16,16]{1,0:T(8,128)(2,1)S(1)}, bf16[16,16]{1,0:T(8,128)(2,1)}, u32[]{:S(2)}) copy-start(bf16[16,16]{1,0:T(8,128)(2,1)} %local_ref.1) | copy-start | bytes 1540
  3.2 10.7 %collective-permute-start = (f32[512,256]{1,0:T(8,128)S(1)}, f32[512,256]{1,0:T(8,128)S(1)}, u32[]{:S(2)}, u32[]{:S(2)}) collective-permute-start(f32[512,256]{1,0:T(8,128)S(1)} %get-tuple-element.14), channel_id=1, source_target_pairs={{0,16},{16,0},{1,17},{17,1},{2,18},{18,2},{3,19},{19,3},{4,20},{20... | collective-permute-start | bytes 1572872 | tf_op jit(solution)/shard_map/ppermute | solution.py:465
  13.8 32.7 %copy-start.1 = (f32[1,2,8192]{2,1,0:T(2,128)S(1)}, f32[1,2,8192]{2,1,0:T(2,128)}, u32[]{:S(2)}) copy-start(f32[1,2,8192]{2,1,0:T(2,128)} %param.9) | copy-start | bytes 196612
  13.9 32.7 %copy-start.2 = (f32[1,2,512]{2,1,0:T(2,128)S(1)}, f32[1,2,512]{2,1,0:T(2,128)}, u32[]{:S(2)}) copy-start(f32[1,2,512]{2,1,0:T(2,128)} %param.8) | copy-start | bytes 12292
  14.8 64.5 %copy-start = (bf16[2,2,256,1024]{3,2,1,0:T(8,128)(2,1)S(1)}, bf16[2,2,256,1024]{3,2,1,0:T(8,128)(2,1)}, u32[]{:S(2)}) copy-start(bf16[2,2,256,1024]{3,2,1,0:T(8,128)(2,1)} %constant.2.clone.depth_ref) | copy-start | bytes 6291460
  76.9 4.3 %collective-permute-start.1 = (bf16[2048,128]{1,0:T(8,128)(2,1)S(1)}, bf16[2048,128]{1,0:T(8,128)(2,1)S(1)}, u32[]{:S(2)}, u32[]{:S(2)}) collective-permute-start(bf16[2048,128]{1,0:T(8,128)(2,1)S(1)} %bitcast.13), channel_id=1, source_target_pairs={{0,16},{16,0},{1,17},{17,1},{2,18},{18,2},{3,19},{19,3},{4,20},{20... | collective-permute-start | bytes 1572872 | tf_op jit(solution)/shard_map/ppermute | solution.py:523
